TPU v7x, 128 devices: a whole 4x4x4 slice. The times are simulated.
128 devices in a mesh: seq: 16 (over z, x), tp: 8 (over y, core).
Axes of the slice: x: 4, y: 4, z: 4, core: 2. Of those that a mesh axis runs over, the one named last changes fastest.
Arguments:
- inner_x: bfloat16 [4, 2048, 8192], P(None, 'seq', 'tp'), may hold values from -6 to 6
- inner_z: bfloat16 [4, 2048, 8192], P(None, 'seq', 'tp'), may hold values from -6 to 6
- conv_tail: bfloat16 [4, 3, 8192], P(None, None, 'tp'), may hold values from -6 to 6
- conv_weight: float32 [4, 8192], P(None, 'tp'), may hold values from -3 to 3
- conv_bias: float32 [8192], P('tp'), may hold values from -3 to 3
- xproj_dt: bfloat16 [8192, 512], P('tp'), may hold values from -0.0625 to 0.0625
- xproj_bc: bfloat16 [8192, 32], P('tp'), may hold values from -0.0625 to 0.0625
- dt_weight: bfloat16 [512, 8192], P(None, 'tp'), may hold values from -0.25 to 0.25
- dt_bias: float32 [8192], P('tp'), may hold values from -5 to -4
- decay_log: float32 [16, 8192], P(None, 'tp'), may hold values from -8 to 1.1
- skip_gain: float32 [8192], P('tp'), may hold values from 0.5 to 1.5
- out_weight: bfloat16 [8192, 8192], P('tp'), may hold values from -0.0625 to 0.0625
- residual: bfloat16 [4, 2048, 8192], P(None, 'seq', 'tp'), may hold values from -6 to 6
- init_state: float32 [4, 16, 8192], P(None, None, 'tp'), may hold values from -6 to 6
Outputs:
- hidden_out: bfloat16 [4, 2048, 8192], P(None, 'seq', 'tp')
- block_states: float32 [16, 4, 16, 8192], P('seq', None, None, 'tp')
All inputs are finite; a program needn't handle non-finite values.
Results may differ from a plain program's by a relative error of at most 0.024.
Values may be sent and summed in bfloat16 or wider, within the bound.
A program may use at most 128 MiB of HBM per device.

v0:
```python
import jax
import jax.numpy as jnp
from jax import lax
from jax.sharding import Mesh
from jax.sharding import PartitionSpec as P

SEQ = ("seq_0", "seq_1")


def passed_along(block, axis, distance):
    devices = range(lax.axis_size(axis))
    route = [(i - distance, i) for i in devices if i - distance in devices]
    return lax.ppermute(block, axis, route)


def gathered_total(x, axis):
    parts = lax.all_gather(x, axis).astype(jnp.float32)
    return parts.sum(axis=0)


def nothing_yet(x, identity):
    return jax.tree.map(
        lambda a, e: jnp.broadcast_to(jnp.asarray(e, a.dtype), a.shape), x, identity
    )


def prefix_by_axis(x, axes, combine, identity):
    before = start = nothing_yet(x, identity)
    running = x
    for axis in reversed(axes):
        length, place = (lax.axis_size(axis), lax.axis_index(axis))
        pieces = jax.tree.map(
            lambda part, kind: lax.all_gather(part.astype(kind), axis),
            running,
            (jnp.bfloat16, jnp.bfloat16),
        )
        inside, running = (start, start)
        for k in range(length):
            passed = k < place
            running = combine(
                running, jax.tree.map(lambda part, own: part[k].astype(own.dtype), pieces, x)
            )
            inside = jax.tree.map(lambda new, old: jnp.where(passed, new, old), running, inside)
        before = combine(inside, before)
    return before


def run_chain(initial, decay_rates, steps_dt, inputs_x, gates_b, reads_c):

    def advance(carried, packed):
        step_dt, value_x, gate_b, read_c = packed
        factor = jnp.exp(decay_rates[None, :, :] * step_dt[:, None, :])
        carried = factor * carried + (step_dt * value_x)[:, None, :] * gate_b[:, :, None]
        emitted = jnp.sum(read_c[:, :, None] * carried, axis=1)
        return (carried, emitted)

    return lax.scan(advance, initial, (steps_dt, inputs_x, gates_b, reads_c), unroll=8)


def compose(earlier_pair, later_pair):
    return (earlier_pair[0] * later_pair[0], later_pair[0] * earlier_pair[1] + later_pair[1])


def body(
    inner_x,
    inner_z,
    conv_tail,
    conv_weight,
    conv_bias,
    xproj_dt,
    xproj_bc,
    dt_weight,
    dt_bias,
    decay_log,
    skip_gain,
    out_weight,
    residual,
    init_state,
):
    kernel = conv_weight.shape[0]
    length = inner_x.shape[1]
    rim_tokens = inner_x[:, length - (kernel - 1) :, :]
    arrived = passed_along(rim_tokens, SEQ, 1)
    earlier = jnp.where(lax.axis_index(SEQ) == 0, conv_tail, arrived)
    joined = jnp.concatenate([earlier, inner_x], axis=1).astype(jnp.float32)
    conv_mixed = conv_bias + conv_weight[0] * joined[:, 0:length, :]
    for offset in range(1, kernel):
        conv_mixed = conv_mixed + conv_weight[offset] * joined[:, offset : offset + length, :]
    conv_act = jax.nn.silu(conv_mixed).astype(jnp.bfloat16)
    low_part = jnp.dot(conv_act, xproj_dt, preferred_element_type=jnp.float32)
    bc_part = jnp.dot(conv_act, xproj_bc, preferred_element_type=jnp.float32)
    low_rank, bc_proj = (
        gathered_total(low_part.astype(jnp.bfloat16), "tp").astype(jnp.float32),
        gathered_total(bc_part.astype(jnp.bfloat16), "tp").astype(jnp.float32),
    )
    normed = (
        low_rank * lax.rsqrt(jnp.mean(low_rank * low_rank, axis=-1, keepdims=True) + 1e-06)
    ).astype(jnp.bfloat16)
    steps_dt = jax.nn.softplus(
        jnp.dot(normed, dt_weight, preferred_element_type=jnp.float32) + dt_bias
    )
    states_n = init_state.shape[1]
    gates_b = bc_proj[..., :states_n]
    reads_c = bc_proj[..., states_n:]
    decay_rates = -jnp.exp(decay_log)
    values = conv_act.astype(jnp.float32)
    flipped = [
        jnp.transpose(array_in, (1, 0, 2)) for array_in in (steps_dt, values, gates_b, reads_c)
    ]
    zeros_state = jnp.zeros_like(init_state)
    ones_state = jnp.ones_like(init_state)
    local_end, local_out = run_chain(
        zeros_state, decay_rates, flipped[0], flipped[1], flipped[2], flipped[3]
    )
    elapsed = jnp.sum(steps_dt, axis=1)
    through = jnp.exp(decay_rates[None, :, :] * elapsed[:, None, :])
    prior_decay, prior_state = prefix_by_axis(
        (through, local_end), SEQ, compose, (ones_state, zeros_state)
    )
    entering = prior_decay * init_state + prior_state
    cumulative = jnp.cumsum(flipped[0], axis=0)
    emitted = local_out
    for state_index in range(states_n):
        emitted = (
            emitted
            + flipped[3][:, :, state_index : state_index + 1]
            * jnp.exp(decay_rates[state_index] * cumulative)
            * entering[:, state_index, :][None]
        )
    final_state = through * entering + local_end
    scanned = jnp.transpose(emitted, (1, 0, 2)) + skip_gain * values
    gated_out = (scanned * jax.nn.silu(inner_z.astype(jnp.float32))).astype(jnp.bfloat16)
    partial_terms = jnp.dot(gated_out, out_weight, preferred_element_type=jnp.float32)
    summed = lax.psum_scatter(
        partial_terms.astype(jnp.bfloat16), "tp", scatter_dimension=2, tiled=True
    ).astype(jnp.float32)
    hidden_out = (residual.astype(jnp.float32) + summed).astype(jnp.bfloat16)
    return (hidden_out, final_state[None])


def solution(mesh):
    finer = Mesh(mesh.devices.reshape(4, 4, mesh.shape["tp"]), ("seq_0", "seq_1", "tp"))
    in_specs = (
        P(None, SEQ, "tp"),
        P(None, SEQ, "tp"),
        P(None, None, "tp"),
        P(None, "tp"),
        P("tp"),
        P("tp", None),
        P("tp", None),
        P(None, "tp"),
        P("tp"),
        P(None, "tp"),
        P("tp"),
        P("tp", None),
        P(None, SEQ, "tp"),
        P(None, None, "tp"),
    )
    out_specs = (P(None, SEQ, "tp"), P(SEQ, None, None, "tp"))
    return jax.shard_map(body, mesh=finer, in_specs=in_specs, out_specs=out_specs, check_vma=False)
```

profile of v0, /device:TPU:1, one launch (start us, length us, event | category | flops | bytes accessed | tf_op | source)
XLA Modules:
  0.0 309.4 jit_solution(3240483556225204636)
XLA Ops:
  8.2 3.9 %collective-permute-start = (bf16[4,3,1024]{2,1,0:T(4,128)(2,1)S(1)}, bf16[4,3,1024]{2,1,0:T(4,128)(2,1)S(1)}, u32[]{:S(2)}, u32[]{:S(2)}) collective-permute-start(bf16[4,3,1024]{2,1,0:T(4,128)(2,1)S(1)} %slice.354), channel_id=1, source_target_pairs={{0,8},{8,16},{16,24},{24,32},{32,40},{40,48},{48,56},{56,64},{64,7... | collective-permute-start | bytes 73736 | tf_op jit(solution)/shard_map/ppermute | solution.py:13
  15.5 2.7 convert_bitcast_fusion
  20.3 14.7 %all-gather.1 = bf16[32,128,32]{1,2,0:T(8,128)(2,1)S(1)} all-gather(bf16[4,128,32]{1,2,0:T(8,128)(2,1)S(1)} %convolution_convert_fusion.1), channel_id=3, replica_groups=mesh['seq_0'=4,'seq_1'=4,'tp'=8] {'tp'}, dimensions={0}, use_global_device_ids=true | all-gather | bytes 294912 | tf_op jit(solution)/shard_map/all_gather | solution.py:17
  37.4 19.1 %all-gather.5.cloned.1.call-done = bf16[32,128,512]{2,1,0:T(8,128)(2,1)} async-done(((bf16[4,128,512]{2,1,0:T(8,128)(2,1)}), bf16[32,128,512]{2,1,0:T(8,128)(2,1)}) %all-gather.5.cloned.1.call-update) | async-done | bytes 4194320 | tf_op jit(solution)/shard_map/all_gather | solution.py:17
  56.5 2.9 convert_reduce_fusion
  61.2 2.7 fusion.43
  63.9 102.4 %while.13 = (s32[]{:T(128)}, f32[4,16,1024]{2,1,0:T(8,128)S(1)}, f32[16,8,4,1024]{3,1,0,2:T(8,128)}, f32[16,1024]{1,0:T(8,128)S(1)}, f32[16,8,4,1024]{3,1,0,2:T(...) while((s32[]{:T(128)}, f32[4,16,1024]{2,1,0:T(8,128)S(1)}, ...), condition=%wide.region_12.13_spmd.clone, body=%wide.region_3.12_spmd.clone.sunk | while | flops 4849674 | bytes 3815240 | solution.py:57
  65.2 2.4 constant_dynamic-slice_fusion.35
  71.4 2.6 constant_dynamic-slice_fusion.35
  77.9 2.7 constant_dynamic-slice_fusion.35
  90.6 2.5 constant_dynamic-slice_fusion.35
  103.2 2.7 constant_dynamic-slice_fusion.35
  116.0 2.7 constant_dynamic-slice_fusion.35
  122.5 2.6 constant_dynamic-slice_fusion.35
  128.9 2.8 constant_dynamic-slice_fusion.35
  154.1 2.9 constant_dynamic-slice_fusion.35
  160.8 2.9 constant_dynamic-slice_fusion.35
  168.1 11.1 %all_gather.34 = bf16[4,4,16,1024]{3,2,1,0:T(8,128)(2,1)S(1)} all-gather(bf16[1,4,16,1024]{3,2,1,0:T(8,128)(2,1)S(1)} %exponential_convert_fusion), channel_id=1, replica_groups=mesh['seq_0'=4,'seq_1'=4,'tp'=8] {'seq_1'}, dimensions={0}, use_global_device_ids=true | all-gather | bytes 655360 | tf_op jit(solution)/shard_map/all_gather | solution.py:33
  179.2 10.1 %all-gather.2 = bf16[16,16,1024]{2,1,0:T(8,128)(2,1)S(1)} all-gather(bf16[4,16,1024]{2,1,0:T(8,128)(2,1)S(1)} %convert_element_type.218), channel_id=4, replica_groups=mesh['seq_0'=4,'seq_1'=4,'tp'=8] {'seq_1'}, dimensions={0}, use_global_device_ids=true | all-gather | bytes 655360 | tf_op jit(solution)/shard_map/all_gather | solution.py:33
  189.5 10.4 %all_gather.35 = bf16[4,4,16,1024]{3,2,1,0:T(8,128)(2,1)S(1)} all-gather(bf16[1,4,16,1024]{3,2,1,0:T(8,128)(2,1)S(1)} %get-tuple-element.184), channel_id=1, replica_groups=mesh['seq_0'=4,'seq_1'=4,'tp'=8] {'seq_0'}, dimensions={0}, use_global_device_ids=true | all-gather | bytes 655360 | tf_op jit(solution)/shard_map/all_gather | solution.py:33
  199.9 11.0 %all_gather.38 = bf16[4,4,16,1024]{3,2,1,0:T(8,128)(2,1)S(1)} all-gather(bf16[1,4,16,1024]{3,2,1,0:T(8,128)(2,1)S(1)} %get-tuple-element.185), channel_id=1, replica_groups=mesh['seq_0'=4,'seq_1'=4,'tp'=8] {'seq_0'}, dimensions={0}, use_global_device_ids=true | all-gather | bytes 655360 | tf_op jit(solution)/shard_map/all_gather | solution.py:33
  213.3 26.0 %fusion.11 = bf16[4,128,8192]{2,1,0:T(8,128)(2,1)} fusion(bf16[1024,8192]{1,0:T(8,128)(2,1)} %param.27, bf16[4,128,1024]{2,1,0:T(8,128)(2,1)S(1)} %copy-done.2, bf16[4,128,1024]{2,1,0:T(8,128)(2,1)S(1)} %copy-done.25, f32[16,8,4,1024]{3,1,0,2:T(8,128)} %get-tuple-element.45, f32[128,4,1024]{2,1,0:T(4,128)S(1)} %copy-done.4, f32[1024]{0:T(1024)S(1)} %copy-done.26, ...), kind=kOutput, calls=%fused_computation.84 | convolution fusion | flops 8632926208 | bytes 31821824 | tf_op jit(solution)/shard_map/dot_general | solution.py:133
  239.3 60.6 %reduce-scatter.2.cloned.1.call-done = bf16[4,128,1024]{2,1,0:T(8,128)(2,1)} async-done(((bf16[4,128,8192]{2,1,0:T(8,128)(2,1)}), bf16[4,128,1024]{2,1,0:T(8,128)(2,1)}) %reduce-scatter.2.cloned.1.call-update) | async-done | bytes 1048592 | tf_op jit(solution)/shard_map/reduce_scatter | solution.py:134
  299.9 2.6 add_convert_fusion
  (562 shorter events, 87.5 us)
Async XLA Ops:
  7.2 52.4 %copy-start = (bf16[512,1024]{1,0:T(8,128)(2,1)S(1)}, bf16[512,1024]{1,0:T(8,128)(2,1)}, u32[]{:S(2)}) copy-start(bf16[512,1024]{1,0:T(8,128)(2,1)} %param.23) | copy-start | bytes 3145732
  7.2 8.3 %copy-start.10 = (f32[1024]{0:T(1024)S(1)}, f32[1024]{0:T(1024)}, u32[]{:S(2)}) copy-start(f32[1024]{0:T(1024)} %param.20) | copy-start | bytes 12292
  7.2 49.3 %all-gather.5.cloned.1.call-start = ((), (), s32[]{:S(2)}) async-start(), calls=%async_computation.2 | async-start | bytes 4718592 | tf_op jit(solution)/shard_map/all_gather | solution.py:17
  8.2 5.0 %collective-permute-start = (bf16[4,3,1024]{2,1,0:T(4,128)(2,1)S(1)}, bf16[4,3,1024]{2,1,0:T(4,128)(2,1)S(1)}, u32[]{:S(2)}, u32[]{:S(2)}) collective-permute-start(bf16[4,3,1024]{2,1,0:T(4,128)(2,1)S(1)} %slice.354), channel_id=1, source_target_pairs={{0,8},{8,16},{16,24},{24,32},{32,40},{40,48},{48,56},{56,64},{64,7... | collective-permute-start | bytes 73736 | tf_op jit(solution)/shard_map/ppermute | solution.py:13
  15.5 2.7 copy-start.24
  19.7 280.2 %reduce-scatter.2.cloned.1.call-start = ((), (), s32[]{:S(2)}) async-start(), calls=%async_computation.1 | async-start | bytes 9437184 | tf_op jit(solution)/shard_map/reduce_scatter | solution.py:134
  56.5 3.1 copy-start.9
  61.2 2.7 copy-start.3
  168.0 42.9 %copy-start.6 = (f32[4,16,1024]{2,1,0:T(8,128)S(1)}, f32[4,16,1024]{2,1,0:T(8,128)}, u32[]{:S(2)}) copy-start(f32[4,16,1024]{2,1,0:T(8,128)} %param.29) | copy-start | bytes 786436
  210.9 2.0 copy-start.4
  210.9 2.0 copy-start.11
  211.0 2.0 copy-start.12
  211.0 2.0 copy-start.13
  211.0 2.0 copy-start.14
  211.0 2.0 copy-start.15
  211.0 2.0 copy-start.16
  211.0 2.0 copy-start.17
  211.0 2.0 copy-start.18
  211.0 2.0 copy-start.19
  211.0 2.0 copy-start.20
  211.0 2.0 copy-start.21
  211.1 2.2 copy-start.25
  211.1 2.2 copy-start.26
  239.3 60.7 %copy-start.5 = (bf16[4,128,1024]{2,1,0:T(8,128)(2,1)S(1)}, bf16[4,128,1024]{2,1,0:T(8,128)(2,1)}, u32[]{:S(2)}) copy-start(bf16[4,128,1024]{2,1,0:T(8,128)(2,1)} %param.28) | copy-start | bytes 3145732
  (6 other events, 10.9 us)
Sparse Core Ops, SparseCore 0:
  19.8 36.5 all-gather.4
  239.4 60.4 reduce-scatter.1
where the time goes:
time: 312 us; the launch traced here: 309 us
  local copies, waits for them, and re-layouts  79.9 us (26%)
  waiting for transfers between devices  79.8 us (26%)
  blocking collectives  57.3 us (18%)
  other arithmetic  41.3 us (13%)
  matrix products  29.6 us (9%)
  between operations  14.6 us (5%)
  starting transfers between devices  4.03 us (1%)
    slice x32, local copies, waits for them, and re-layouts, run_chain(): lax.scan(advance, initial, (steps_dt, inputs_x, gates_b, reads_c), unroll=8)  61 us
    reduce_scatter x1, waiting for transfers between devices, body(): lax.psum_scatter(partial_terms.astype(jnp.bfloat16), 'tp', scatter_dimens...  60.6 us
    all_gather x4, blocking collectives, prefix_by_axis(): lax.all_gather(part.astype(kind), axis)  42.6 us
    dot_general x1, matrix products, body(): jnp.dot(gated_out, out_weight, preferred_element_type=jnp.float32)  26 us
    reduce_sum x48, other arithmetic, advance(): emitted = jnp.sum(read_c[:, :, None] * carried, axis=1)  23.5 us
    all_gather x1, waiting for transfers between devices, gathered_total(): parts = lax.all_gather(x, axis).astype(jnp.float32)  19.1 us
    all_gather x1, blocking collectives, gathered_total(): parts = lax.all_gather(x, axis).astype(jnp.float32)  14.7 us
    dynamic_update_slice x16, local copies, waits for them, and re-layouts, run_chain(): lax.scan(advance, initial, (steps_dt, inputs_x, gates_b, reads_c), unroll=8)  12.1 us
  transfers between devices with their start and end apart: 3, of which 3 were waited for; matrix products, arithmetic and copies ran while one was open for 1% of the time, Pallas kernels for 0%

commit v1 on v0

v1 whole, which is shorter than its diff:
```python
import jax
import jax.numpy as jnp
from jax import lax
from jax.experimental import pallas as pl
from jax.experimental.pallas import tpu as pltpu
from jax.sharding import PartitionSpec as P

MESH = pl.DeviceIdType.MESH
F32 = jnp.float32
BF16 = jnp.bfloat16
LOG2E = 1.4426950408889634

N_SEQ = 16
N_TP = 8
N_Y = 4
SEQS = 4
TOK = 128
CH = 1024
NG = CH // 128
RANK = 512
LOWW = RANK + 128
NS = 16
GROUPS = 2
GS = SEQS // GROUPS
OWN = TOK // N_TP
ROWS = SEQS * TOK
GROWS = GS * TOK
HALF = TOK // 2


def mix_kernel(
    x_ref,
    tail_ref,
    cw_ref,
    cb_ref,
    xdt_ref,
    xbc_ref,
    dtb_ref,
    decay_ref,
    skip_ref,
    init_ref,
    z_hbm,
    dtw_hbm,
    w_hbm,
    res_hbm,
    out_ref,
    st_ref,
    z_ref,
    dtw_ref,
    w_ref,
    res_ref,
    rim_out,
    rim_in,
    joined,
    act,
    xg,
    dtg,
    splat,
    rate_t,
    init_t,
    flip,
    lowp,
    lowr,
    lown,
    exs,
    exr,
    rets,
    ent,
    snd,
    rcv,
    opp,
    fin,
    load_sem,
    rim_ssem,
    rim_rsem,
    low_ssem,
    low_rsem,
    nrm_ssem,
    nrm_rsem,
    ex_ssem,
    ex_rsem,
    ret_ssem,
    ret_rsem,
    sib_ssem,
    sib_rsem,
    opp_ssem,
    opp_rsem,
    fin_ssem,
    fin_rsem,
):
    q = lax.axis_index("seq")
    t = lax.axis_index("tp")
    y = t // 2
    core = lax.rem(t, 2)

    def on_tp(p):
        return (q, p)

    def on_seq(p):
        return (p, t)

    sib = on_tp(y * 2 + 1 - core)
    up = on_tp(lax.rem(y + 1, N_Y) * 2 + core)
    down = on_tp(lax.rem(y + N_Y - 1, N_Y) * 2 + core)

    def remote(src, dst, ssem, rsem, dev):
        return pltpu.make_async_remote_copy(
            src_ref=src, dst_ref=dst, send_sem=ssem, recv_sem=rsem, device_id=dev, device_id_type=MESH
        )

    loads = [
        pltpu.make_async_copy(dtw_hbm, dtw_ref, load_sem.at[0]),
        pltpu.make_async_copy(z_hbm, z_ref, load_sem.at[1]),
        pltpu.make_async_copy(w_hbm, w_ref, load_sem.at[2]),
        pltpu.make_async_copy(res_hbm, res_ref, load_sem.at[3]),
    ]
    for c in loads:
        c.start()

    barrier = pltpu.get_barrier_semaphore()
    for k in range(1, N_TP):
        pl.semaphore_signal(barrier, inc=1, device_id=on_tp(lax.rem(t + k, N_TP)), device_id_type=MESH)
    for k in range(1, N_SEQ):
        pl.semaphore_signal(barrier, inc=1, device_id=on_seq(lax.rem(q + k, N_SEQ)), device_id_type=MESH)

    row8 = lax.broadcasted_iota(jnp.int32, (8, CH), 0)
    last = [x_ref[s, TOK - 16 : TOK, :].astype(F32)[8:16, :] for s in range(SEQS)]
    packed = [jnp.where(row8 < 4, pltpu.roll(last[s], 4, 0), last[s + 1]) for s in (0, 2)]
    rim_out[...] = jnp.concatenate(packed, axis=0).astype(BF16)

    pl.semaphore_wait(barrier, N_TP - 1 + N_SEQ - 1)
    rim = remote(rim_out, rim_in, rim_ssem, rim_rsem, on_seq(lax.rem(q + 1, N_SEQ)))
    rim.start()

    for g in range(GROUPS):
        lowp[g * GROWS : (g + 1) * GROWS, RANK:] = jnp.zeros((GROWS, LOWW - RANK), BF16)

    for nb in range(NS // 8):
        for c in range(NG):
            flip[c * 8 : (c + 1) * 8, :] = -jnp.exp(decay_ref[nb * 8 : nb * 8 + 8, c * 128 : (c + 1) * 128]) * LOG2E
        for i in range(8):
            rate_t[nb * 8 + i] = flip[pl.ds(i, 8, stride=8), :]

    @pl.loop(0, SEQS)
    def _(s):
        for nb in range(NS // 8):
            for c in range(NG):
                flip[c * 8 : (c + 1) * 8, :] = init_ref[s, nb * 8 : nb * 8 + 8, c * 128 : (c + 1) * 128]
            for i in range(8):
                init_t[s, nb * 8 + i] = flip[pl.ds(i, 8, stride=8), :]

    def widen(s):
        @pl.loop(0, TOK // 16)
        def _(b):
            r = pl.multiple_of(b * 16, 16)
            joined[s, pl.ds(r + 8, 16), :] = x_ref[s, pl.ds(r, 16), :].astype(F32)

    def conv_block(s, b):
        r = pl.multiple_of(b * 16, 16)
        window = joined[s, pl.ds(r, 24), :]
        mixed = cb_ref[...] + cw_ref[0:1, :] * window[5:21, :]
        for k in range(1, 4):
            mixed = mixed + cw_ref[k : k + 1, :] * window[5 + k : 21 + k, :]
        rounded = (mixed / (1.0 + jnp.exp(-mixed))).astype(BF16)
        act[pl.ds(s * TOK + r, 16), :] = rounded
        wide = rounded.astype(F32)
        for h in range(2):
            base = pl.multiple_of((s * (TOK // 8) + b * 2 + h) * 64, 64)
            for c in range(NG):
                xg[pl.ds(base + c * 8, 8), :] = wide[h * 8 : h * 8 + 8, c * 128 : (c + 1) * 128]

    def low_copy(g, k):
        p = lax.rem(t + k, N_TP)
        return [
            remote(
                lowp.at[pl.ds((g * GS + s) * TOK + pl.multiple_of(p * OWN, OWN), OWN), :],
                lowr.at[g, k - 1, s],
                low_ssem.at[g, k - 1, s],
                low_rsem.at[g, k - 1, s],
                on_tp(p),
            )
            for s in range(GS)
        ]

    def nrm_copy(g, k):
        p = lax.rem(t + k, N_TP)
        out = []
        for s in range(GS):
            rows = pl.ds((g * GS + s) * TOK + pl.multiple_of(t * OWN, OWN), OWN)
            out.append(
                remote(
                    lown.at[rows, :], lown.at[rows, :], nrm_ssem.at[g, k - 1, s], nrm_rsem.at[g, k - 1, s], on_tp(p)
                )
            )
        return out

    def ex_copy(g, k):
        p = lax.rem(q + k, N_SEQ)
        return remote(exs.at[g, p], exr.at[g, q], ex_ssem.at[g, k - 1], ex_rsem.at[g, k - 1], on_seq(p))

    def ret_copy(g, k):
        p = lax.rem(q + k, N_SEQ)
        return remote(rets.at[g, p], ent.at[g, q], ret_ssem.at[g, k - 1], ret_rsem.at[g, k - 1], on_seq(p))

    for g in range(GROUPS):
        for s in range(g * GS, (g + 1) * GS):
            widen(s)

            @pl.loop(1, TOK // 16)
            def _(b):
                conv_block(s, b)

        if g == 0:
            rim.wait()
            for s in range(SEQS):
                part = rim_in[...].astype(F32)[(s // 2) * 8 : (s // 2) * 8 + 8, :]
                joined[s, 0:8, :] = pltpu.roll(part, 4, 0) if s % 2 == 0 else part

            @pl.when(q == 0)
            def _():
                for s in range(SEQS):
                    joined[s, 5:8, :] = tail_ref[s].astype(F32)

        for s in range(g * GS, (g + 1) * GS):
            conv_block(s, 0)
        rows = slice(g * GROWS, (g + 1) * GROWS)
        lowp[rows, 0:RANK] = jnp.dot(act[rows, :], xdt_ref[...], preferred_element_type=F32).astype(BF16)
        lowp[rows, RANK : RANK + 2 * NS] = jnp.dot(
            act[rows, :], xbc_ref[...], preferred_element_type=F32
        ).astype(BF16)
        for k in range(1, N_TP):
            for c in low_copy(g, k):
                c.start()

    for g in range(GROUPS):
        for k in range(1, N_TP):
            for c in low_copy(g, k):
                c.wait_recv()
        for s in range(GS):
            rows = pl.ds((g * GS + s) * TOK + pl.multiple_of(t * OWN, OWN), OWN)
            total = lowp[rows, :].astype(F32)
            for k in range(N_TP - 1):
                total = total + lowr[g, k, s].astype(F32)
            low = total[:, :RANK]
            scale = lax.rsqrt(jnp.mean(low * low, axis=-1, keepdims=True) + 1e-6)
            lown[rows, 0:RANK] = (low * scale).astype(BF16)
            bc = total[:, RANK:]
            high = bc.astype(BF16).astype(F32)
            lown[rows, RANK:] = (high + pltpu.roll(bc - high, 2 * NS, 1)).astype(BF16)
        for k in range(1, N_TP):
            for c in nrm_copy(g, k):
                c.start()

    loads[0].wait()

    def steps(g):
        base = g * GROWS

        @pl.loop(0, CH // 256)
        def _(nc):
            cols = pl.ds(pl.multiple_of(nc * 256, 256), 256)
            pre = (
                jnp.dot(lown[base : base + GROWS, 0:RANK], dtw_ref[:, cols], preferred_element_type=F32)
                + dtb_ref[:, cols]
            )
            dt = jnp.maximum(pre, 0.0) + jnp.log1p(jnp.exp(-jnp.abs(pre)))
            for b in range(GROWS // 8):
                for h in range(2):
                    at = pl.multiple_of((base // 8 + b) * 64 + (nc * 2 + h) * 8, 8)
                    dtg[pl.ds(at, 8), :] = dt[b * 8 : b * 8 + 8, h * 128 : (h + 1) * 128]

        @pl.loop(0, NS)
        def _(p):
            r = lax.broadcasted_iota(jnp.int32, (128, 256), 0)
            n = lax.broadcasted_iota(jnp.int32, (128, 256), 1) // 128 + 2 * p
            pick = jnp.where((r == n) | (r == n + 2 * NS), 1.0, 0.0).astype(BF16)
            wide = jnp.dot(lown[base : base + GROWS, RANK:], pick, preferred_element_type=F32)
            for h in range(2):
                at = pl.multiple_of((2 * p + h) * ROWS + base, GROWS)
                splat[pl.ds(at, GROWS), :] = wide[:, h * 128 : h * 128 + 128]

    def first_pass(g, sl):
        s = g * GS + sl
        rates = [rate_t[n] for n in range(NS)]

        def block(b, carry):
            h, elapsed = list(carry[0]), carry[1]
            base = pl.multiple_of((s * (TOK // 8) + b) * 64, 64)
            for i in range(8):
                dt = dtg[pl.ds(base + i, 8, stride=8), :]
                u = dt * xg[pl.ds(base + i, 8, stride=8), :]
                elapsed = elapsed + dt
                tok = s * TOK + b * 8 + i
                for n in range(NS):
                    h[n] = jnp.exp2(rates[n] * dt) * h[n] + splat[pl.ds(n * ROWS + tok, 1), :] * u
            return (tuple(h), elapsed)

        zero = jnp.zeros((8, 128), F32)
        h, elapsed = lax.fori_loop(0, TOK // 8, block, ((zero,) * NS, zero))
        for n in range(NS):
            pair = jnp.concatenate([h[n], jnp.exp2(rates[n] * elapsed)], axis=0).astype(BF16)
            exs[g, n, sl * 16 : (sl + 1) * 16, :] = pair

    for g in range(GROUPS):
        for k in range(1, N_TP):
            for c in nrm_copy(g, k):
                c.wait_recv()
        steps(g)
        for sl in range(GS):
            first_pass(g, sl)
        exr[g, q] = exs[g, q]
        for k in range(1, N_SEQ):
            ex_copy(g, k).start()

    for g in range(GROUPS):
        for k in range(1, N_SEQ):
            ex_copy(g, k).wait_recv()
        for sl in range(GS):
            h = init_t[g * GS + sl, q]
            for i in range(N_SEQ):
                rets[g, i, sl * 8 : sl * 8 + 8, :] = h
                pair = exr[g, i, sl * 16 : (sl + 1) * 16, :].astype(F32)
                h = pair[8:16] * h + pair[0:8]
        ent[g, q] = rets[g, q]
        for k in range(1, N_SEQ):
            ret_copy(g, k).start()

    def second_pass(s):
        g, sl = s // GS, s % GS
        rates = [rate_t[n] for n in range(NS)]
        skip = skip_ref[...]

        def block(b, h):
            h = list(h)
            base = pl.multiple_of((s * (TOK // 8) + b) * 64, 64)
            for i in range(8):
                dt = dtg[pl.ds(base + i, 8, stride=8), :]
                v = xg[pl.ds(base + i, 8, stride=8), :]
                u = dt * v
                tok = s * TOK + b * 8 + i
                total = skip * v
                for n in range(NS):
                    h[n] = jnp.exp2(rates[n] * dt) * h[n] + splat[pl.ds(n * ROWS + tok, 1), :] * u
                    total = total + splat[pl.ds((NS + n) * ROWS + tok, 1), :] * h[n]
                xg[pl.ds(base + i, 8, stride=8), :] = total
            return tuple(h)

        h = lax.fori_loop(0, TOK // 8, block, tuple(ent[g, n, sl * 8 : sl * 8 + 8, :] for n in range(NS)))
        for nb in range(NS // 8):
            for i in range(8):
                flip[pl.ds(i, 8, stride=8), :] = h[nb * 8 + i]
            for c in range(NG):
                st_ref[0, s, nb * 8 : nb * 8 + 8, c * 128 : (c + 1) * 128] = flip[c * 8 : (c + 1) * 8, :]

    def gate(s):
        @pl.loop(0, TOK // 16)
        def _(b):
            r = pl.multiple_of(b * 16, 16)
            z = z_ref[s, pl.ds(r, 16), :].astype(F32)
            sz = z / (1.0 + jnp.exp(-z))
            base = pl.multiple_of((s * (TOK // 8) + b * 2) * 64, 64)
            for c in range(NG):
                scanned = jnp.concatenate(
                    [xg[pl.ds(base + c * 8, 8), :], xg[pl.ds(base + 64 + c * 8, 8), :]], axis=0
                )
                act[pl.ds(s * TOK + r, 16), c * 128 : (c + 1) * 128] = (
                    scanned * sz[:, c * 128 : (c + 1) * 128]
                ).astype(BF16)

    def columns(j, who, n):
        dest = lax.rem(y + j, N_Y) * 2 + who
        return pl.ds(pl.multiple_of(dest * CH + n * 256, 256), 256)

    def product(s, j, who, n):
        return jnp.dot(
            act[s * TOK : (s + 1) * TOK, :], w_ref[:, columns(j, who, n)], preferred_element_type=F32
        )

    def sib_copy(s, j):
        return remote(snd.at[s, j], rcv.at[s, j], sib_ssem.at[s, j], sib_rsem.at[s, j], sib)

    lo, hi = pl.ds(0, HALF), pl.ds(HALF, HALF)

    def opp_copies(s):
        return (
            remote(rcv.at[s, 2, lo], opp.at[s, 0], opp_ssem.at[s, 0], opp_rsem.at[s, 0], up),
            remote(rcv.at[s, 2, hi], opp.at[s, 1], opp_ssem.at[s, 1], opp_rsem.at[s, 1], down),
        )

    def own_up(s):
        return remote(rcv.at[s, 1, hi], fin.at[s, 0, hi], fin_ssem.at[s, 0], fin_rsem.at[s, 0], up)

    def own_down(s):
        return remote(rcv.at[s, 3, lo], fin.at[s, 1, lo], fin_ssem.at[s, 1], fin_rsem.at[s, 1], down)

    def fwd_copies(s):
        return (
            remote(rcv.at[s, 1, lo], fin.at[s, 0, lo], fin_ssem.at[s, 2], fin_rsem.at[s, 2], up),
            remote(rcv.at[s, 3, hi], fin.at[s, 1, hi], fin_ssem.at[s, 3], fin_rsem.at[s, 3], down),
        )

    def for_sibling(s):
        for j in (2, 1, 3, 0):

            @pl.loop(0, CH // 256)
            def _(n):
                cols = pl.ds(pl.multiple_of(n * 256, 256), 256)
                snd[s, j, :, cols] = product(s, j, 1 - core, n).astype(BF16)

            sib_copy(s, j).start()

    def for_chip(s):
        for j in (2, 1, 3, 0):
            sib_copy(s, j).wait_recv()

            @pl.loop(0, CH // 256)
            def _(n):
                cols = pl.ds(pl.multiple_of(n * 256, 256), 256)
                rcv[s, j, :, cols] = (product(s, j, core, n) + rcv[s, j, :, cols].astype(F32)).astype(BF16)

            if j == 2:
                for c in opp_copies(s):
                    c.start()
            if j == 1:
                own_up(s).start()
            if j == 3:
                own_down(s).start()

    def forward(s):
        for d, (arriving, c) in enumerate(zip(opp_copies(s), fwd_copies(s))):
            arriving.wait_recv()
            j, r0 = (1, 0) if d == 0 else (3, HALF)

            @pl.loop(0, HALF // 16)
            def _(b):
                r = pl.multiple_of(b * 16, 16)
                mine = rcv[s, j, pl.ds(r0 + r, 16), :].astype(F32)
                rcv[s, j, pl.ds(r0 + r, 16), :] = (mine + opp[s, d, pl.ds(r, 16), :].astype(F32)).astype(BF16)

            c.start()

    def finish(s):
        for c in (own_up(s), own_down(s)) + fwd_copies(s):
            c.wait_recv()

        @pl.loop(0, TOK // 16)
        def _(b):
            r = pl.ds(pl.multiple_of(b * 16, 16), 16)
            total = res_ref[s, r, :].astype(F32) + rcv[s, 0, r, :].astype(F32)
            total = total + fin[s, 0, r, :].astype(F32) + fin[s, 1, r, :].astype(F32)
            out_ref[s, r, :] = total.astype(BF16)

    for s in range(SEQS):
        if s % GS == 0:
            for k in range(1, N_SEQ):
                ret_copy(s // GS, k).wait_recv()
        second_pass(s)
        if s == 0:
            loads[1].wait()
            loads[2].wait()
        gate(s)
        for_sibling(s)
        if s > 0:
            forward(s - 1)
        for_chip(s)
        if s == 1:
            loads[3].wait()
        if s > 1:
            finish(s - 2)
    forward(SEQS - 1)
    finish(SEQS - 2)
    finish(SEQS - 1)

    for g in range(GROUPS):
        for k in range(1, N_TP):
            for c in low_copy(g, k) + nrm_copy(g, k):
                c.wait_send()
        for k in range(1, N_SEQ):
            ex_copy(g, k).wait_send()
            ret_copy(g, k).wait_send()
    for s in range(SEQS):
        for j in range(N_Y):
            sib_copy(s, j).wait_send()
        for c in opp_copies(s) + (own_up(s), own_down(s)) + fwd_copies(s):
            c.wait_send()


def body(
    inner_x,
    inner_z,
    conv_tail,
    conv_weight,
    conv_bias,
    xproj_dt,
    xproj_bc,
    dt_weight,
    dt_bias,
    decay_log,
    skip_gain,
    out_weight,
    residual,
    init_state,
):
    vmem = pl.BlockSpec(memory_space=pltpu.VMEM)
    anym = pl.BlockSpec(memory_space=pl.ANY)
    dma = pltpu.SemaphoreType.DMA
    scratch = [
        pltpu.VMEM((SEQS, TOK, CH), BF16),
        pltpu.VMEM((RANK, CH), BF16),
        pltpu.VMEM((CH, N_TP * CH), BF16),
        pltpu.VMEM((SEQS, TOK, CH), BF16),
        pltpu.VMEM((16, CH), BF16),
        pltpu.VMEM((16, CH), BF16),
        pltpu.VMEM((SEQS, TOK + 8, CH), F32),
        pltpu.VMEM((ROWS, CH), BF16),
        pltpu.VMEM((ROWS * 8, 128), F32),
        pltpu.VMEM((ROWS * 8, 128), F32),
        pltpu.VMEM((2 * NS * ROWS, 128), F32),
        pltpu.VMEM((NS, 8, 128), F32),
        pltpu.VMEM((SEQS, NS, 8, 128), F32),
        pltpu.VMEM((64, 128), F32),
        pltpu.VMEM((ROWS, LOWW), BF16),
        pltpu.VMEM((GROUPS, N_TP - 1, GS, OWN, LOWW), BF16),
        pltpu.VMEM((ROWS, LOWW), BF16),
        pltpu.VMEM((GROUPS, NS, GS * 16, 128), BF16),
        pltpu.VMEM((GROUPS, N_SEQ, GS * 16, 128), BF16),
        pltpu.VMEM((GROUPS, N_SEQ, GS * 8, 128), F32),
        pltpu.VMEM((GROUPS, NS, GS * 8, 128), F32),
        pltpu.VMEM((SEQS, N_Y, TOK, CH), BF16),
        pltpu.VMEM((SEQS, N_Y, TOK, CH), BF16),
        pltpu.VMEM((SEQS, 2, HALF, CH), BF16),
        pltpu.VMEM((SEQS, 2, TOK, CH), BF16),
        dma((4,)),
        dma,
        dma,
        dma((GROUPS, N_TP - 1, GS)),
        dma((GROUPS, N_TP - 1, GS)),
        dma((GROUPS, N_TP - 1, GS)),
        dma((GROUPS, N_TP - 1, GS)),
        dma((GROUPS, N_SEQ - 1)),
        dma((GROUPS, N_SEQ - 1)),
        dma((GROUPS, N_SEQ - 1)),
        dma((GROUPS, N_SEQ - 1)),
        dma((SEQS, N_Y)),
        dma((SEQS, N_Y)),
        dma((SEQS, 2)),
        dma((SEQS, 2)),
        dma((SEQS, 4)),
        dma((SEQS, 4)),
    ]
    return pl.pallas_call(
        mix_kernel,
        out_shape=(
            jax.ShapeDtypeStruct((SEQS, TOK, CH), BF16),
            jax.ShapeDtypeStruct((1, SEQS, NS, CH), F32),
        ),
        in_specs=[vmem] * 10 + [anym] * 4,
        out_specs=(vmem, vmem),
        scratch_shapes=scratch,
        compiler_params=pltpu.CompilerParams(
            collective_id=0, has_side_effects=True, vmem_limit_bytes=62 * 1024 * 1024
        ),
    )(
        inner_x,
        conv_tail,
        conv_weight,
        conv_bias.reshape(1, CH),
        xproj_dt,
        xproj_bc,
        dt_bias.reshape(1, CH),
        decay_log,
        skip_gain.reshape(8, 128),
        init_state,
        inner_z,
        dt_weight,
        out_weight,
        residual,
    )


def solution(mesh):
    in_specs = (
        P(None, "seq", "tp"),
        P(None, "seq", "tp"),
        P(None, None, "tp"),
        P(None, "tp"),
        P("tp"),
        P("tp", None),
        P("tp", None),
        P(None, "tp"),
        P("tp"),
        P(None, "tp"),
        P("tp"),
        P("tp", None),
        P(None, "seq", "tp"),
        P(None, None, "tp"),
    )
    out_specs = (P(None, "seq", "tp"), P("seq", None, None, "tp"))
    return jax.shard_map(body, mesh=mesh, in_specs=in_specs, out_specs=out_specs, check_vma=False)
```

time: 312 us -> 112 us (0.36)
  Pallas kernels: 0 us -> 104 us
  waiting for transfers between devices: 79.8 us -> 0 us
  local copies, waits for them, and re-layouts: 79.9 us -> 6.98 us
  blocking collectives: 57.3 us -> 0 us
  other arithmetic: 41.3 us -> 0 us
  matrix products: 29.6 us -> 0 us
  between operations: 14.6 us -> 0.64 us
  starting transfers between devices: 4.03 us -> 0 us
    pallas_call x0 -> x1, Pallas kernels: none -> 104 us  [body(): pl.pallas_call(mix_kernel, out_shape=(jax.ShapeDtypeStruct((SEQS, TOK, CH...]
    slice x37 -> x0, local copies, waits for them, and re-layouts: 63.7 us -> none  [the longest x32 61 us: run_chain(): lax.scan(advance, initial, (steps_dt, inputs_x, gates_b, reads_c), unroll=8)]
    reduce_scatter x1 -> x0, waiting for transfers between devices: 60.6 us -> none  [body(): lax.psum_scatter(partial_terms.astype(jnp.bfloat16), 'tp', scatter_dimens...]
    all_gather x5 -> x0, blocking collectives: 57.3 us -> none  [the longest x4 42.6 us: prefix_by_axis(): lax.all_gather(part.astype(kind), axis)]
    dot_general x4 -> x0, matrix products: 29.6 us -> none  [the longest x1 26 us: body(): jnp.dot(gated_out, out_weight, preferred_element_type=jnp.float32)]
    reduce_sum x52 -> x0, other arithmetic: 27.9 us -> none  [the longest x48 23.5 us: advance(): emitted = jnp.sum(read_c[:, :, None] * carried, axis=1)]
    all_gather x1 -> x0, waiting for transfers between devices: 19.1 us -> none  [gathered_total(): parts = lax.all_gather(x, axis).astype(jnp.float32)]
    dynamic_update_slice x16 -> x0, local copies, waits for them, and re-layouts: 12.1 us -> none  [run_chain(): lax.scan(advance, initial, (steps_dt, inputs_x, gates_b, reads_c), unroll=8)]
  transfers between devices with their start and end apart: 3 -> 0, of which waited for: 3 -> 0; matrix products, arithmetic and copies ran while one was open for 1% -> 0% of each run, Pallas kernels for 0% -> 0%
where the time goes in v1:
time: 112 us; the launch traced here: 111 us
  Pallas kernels  104 us (93%)
  local copies, waits for them, and re-layouts  6.98 us (6%)
    pallas_call x1, Pallas kernels, body(): pl.pallas_call(mix_kernel, out_shape=(jax.ShapeDtypeStruct((SEQS, TOK, CH...  104 us
    unnamed x4, local copies, waits for them, and re-layouts  6.98 us

profile of v1, /device:TPU:1, one launch (start us, length us, event | category | flops | bytes accessed | tf_op | source)
XLA Modules:
  0.0 111.2 jit_solution(8979480033709816810)
XLA Ops:
  0.6 1.4 %copy.16.tail_ref = bf16[4,3,1024]{2,1,0:T(4,128)(2,1)} copy(bf16[4,3,1024]{2,0,1:T(4,128)(2,1)} %param.16) | data formatting | bytes 49152 | tf_op args[2]
  2.0 1.7 %copy.17.xbc_ref = bf16[1024,32]{1,0:T(8,128)(2,1)} copy(bf16[1024,32]{0,1:T(8,128)(2,1)} %param.20) | data formatting | bytes 131072 | tf_op args[6]
  3.7 103.6 %shard_map.149 = (bf16[4,128,1024]{2,1,0:T(8,128)(2,1)}, f32[1,4,16,1024]{3,2,1,0:T(8,128)}) custom-call(bf16[4,128,1024]{2,1,0:T(8,128)(2,1)} %x_ref.1, bf16[4,3,1024]{2,1,0:T(4,128)(2,1)} %copy.16.tail_ref, f32[4,1024]{1,0:T(4,128)} %cw_ref.1, f32[1,1024]{1,0:T(1,128)} %bitcast.3, bf16[1024,512]{1,0:T(8,128)(2,1)} %xdt_ref.1, ...), custom_call_target="tpu_custom_call" | custom-call | tf_op jit(solution)/shard_map/pallas_call | solution.py:551
  107.3 2.3 %copy.20 = bf16[4,128,1024]{2,1,0:T(8,128)(2,1)} copy(bf16[4,128,1024]{2,1,0:T(8,128)(2,1)} %get-tuple-element.4) | data formatting | bytes 2097152
  109.5 1.7 %copy.21 = f32[1,4,16,1024]{3,2,1,0:T(8,128)} copy(f32[1,4,16,1024]{3,2,1,0:T(8,128)} %get-tuple-element.5) | data formatting | bytes 524288

commit v2 on v1

v2 whole, which is shorter than its diff:
```python
import jax
import jax.numpy as jnp
from jax import lax
from jax.experimental import pallas as pl
from jax.experimental.pallas import tpu as pltpu
from jax.sharding import PartitionSpec as P

MESH = pl.DeviceIdType.MESH
F32 = jnp.float32
BF16 = jnp.bfloat16
LOG2E = 1.4426950408889634

N_SEQ = 16
N_TP = 8
N_X = 4
N_Y = 4
N_Z = 4
SEQS = 4
TOK = 128
CH = 1024
NG = CH // 128
RANK = 512
LOWW = RANK + 128
NS = 16
ROWS = SEQS * TOK
HALF = TOK // 2
OWN = HALF // N_Y
EXROWS = (NS + 2) * 8


def mix_kernel(
    tail_ref,
    cw_ref,
    cb_ref,
    xbc_ref,
    dtb_ref,
    decay_ref,
    skip_ref,
    x_hbm,
    xdt_hbm,
    init_hbm,
    dtw_hbm,
    z_hbm,
    w_hbm,
    res_hbm,
    out_ref,
    st_ref,
    x_ref,
    xdt_ref,
    init_ref,
    dtw_ref,
    z_ref,
    w_ref,
    res_ref,
    rim_out,
    rim_in,
    joined,
    act,
    xg,
    dtg,
    splat,
    pick,
    pre,
    rate_t,
    init_t,
    flip,
    lowp,
    lows,
    lowr,
    lown,
    exx,
    exz,
    before,
    since,
    ent,
    snd,
    rcv,
    opp,
    fin,
    load_sem,
    rim_sem,
    lsib_sem,
    low_sem,
    nrm_sem,
    nsib_sem,
    exx_sem,
    exz_sem,
    sib_sem,
    opp_sem,
    fin_sem,
):
    q = lax.axis_index("seq")
    t = lax.axis_index("tp")
    z, x = q // N_X, lax.rem(q, N_X)
    y, core = t // 2, lax.rem(t, 2)

    sib = (q, y * 2 + 1 - core)

    def at_y(k):
        return (q, lax.rem(y + k, N_Y) * 2 + core)

    def at_x(k):
        return (z * N_X + lax.rem(x + k, N_X), t)

    def at_z(k):
        return (lax.rem(z + k, N_Z) * N_X + x, t)

    up, down = at_y(1), at_y(3)
    after = (lax.rem(q + 1, N_SEQ), t)
    prior = (lax.rem(q + N_SEQ - 1, N_SEQ), t)

    def remote(src, dst, sems, dev):
        return pltpu.make_async_remote_copy(
            src_ref=src, dst_ref=dst, send_sem=sems.at[0], recv_sem=sems.at[1], device_id=dev, device_id_type=MESH
        )

    barrier = pltpu.get_barrier_semaphore()
    peers = [after, prior, sib] + [at_y(k) for k in (1, 2, 3)]
    peers += [at_x(k) for k in (1, 2, 3)] + [at_z(k) for k in (1, 2, 3)]
    loads = [
        pltpu.make_async_copy(src, dst, load_sem.at[i])
        for i, (src, dst) in enumerate(
            (
                (x_hbm, x_ref),
                (xdt_hbm, xdt_ref),
                (init_hbm, init_ref),
                (dtw_hbm, dtw_ref),
                (w_hbm, w_ref),
                (z_hbm, z_ref),
                (res_hbm, res_ref),
            )
        )
    ]
    x_load, xdt_load, init_load, dtw_load, w_load, z_load, res_load = loads
    x_load.start()
    for dev in peers:
        pl.semaphore_signal(barrier, inc=1, device_id=dev, device_id_type=MESH)
    for c in loads[1:]:
        c.start()

    x_load.wait()
    row8 = lax.broadcasted_iota(jnp.int32, (8, CH), 0)
    last = [x_ref[s, TOK - 16 : TOK, :].astype(F32)[8:16, :] for s in range(SEQS)]
    packed = [jnp.where(row8 < 4, pltpu.roll(last[s], 4, 0), last[s + 1]) for s in (0, 2)]
    rim_out[...] = jnp.concatenate(packed, axis=0).astype(BF16)

    pl.semaphore_wait(barrier, len(peers))
    rim = remote(rim_out, rim_in, rim_sem, after)
    rim.start()

    def conv_block(s, b):
        r = pl.multiple_of(b * 16, 16)
        window = joined[s, pl.ds(r, 24), :]
        mixed = cb_ref[...] + cw_ref[0:1, :] * window[5:21, :]
        for k in range(1, 4):
            mixed = mixed + cw_ref[k : k + 1, :] * window[5 + k : 21 + k, :]
        rounded = (mixed / (1.0 + jnp.exp(-mixed))).astype(BF16)
        act[pl.ds(pl.multiple_of(s * TOK + r, 16), 16), :] = rounded
        wide = rounded.astype(F32)
        for h in range(2):
            base = pl.multiple_of((s * (TOK // 8) + b * 2 + h) * 64, 64)
            for c in range(NG):
                xg[pl.ds(base + c * 8, 8), :] = wide[h * 8 : h * 8 + 8, c * 128 : (c + 1) * 128]

    @pl.loop(0, SEQS)
    def _(s):
        @pl.loop(0, TOK // 16)
        def _(b):
            r = pl.multiple_of(b * 16, 16)
            joined[s, pl.ds(r + 8, 16), :] = x_ref[s, pl.ds(r, 16), :].astype(F32)

        @pl.loop(1, TOK // 16)
        def _(b):
            conv_block(s, b)

    for nb in range(NS // 8):
        for c in range(NG):
            flip[c * 8 : (c + 1) * 8, :] = -jnp.exp(decay_ref[nb * 8 : nb * 8 + 8, c * 128 : (c + 1) * 128]) * LOG2E
        for i in range(8):
            rate_t[nb * 8 + i] = flip[pl.ds(i, 8, stride=8), :]

    init_load.wait()

    @pl.loop(0, SEQS)
    def _(s):
        for nb in range(NS // 8):
            for c in range(NG):
                flip[c * 8 : (c + 1) * 8, :] = init_ref[s, nb * 8 : nb * 8 + 8, c * 128 : (c + 1) * 128]
            for i in range(8):
                init_t[s, nb * 8 + i] = flip[pl.ds(i, 8, stride=8), :]

    for n in range(2 * NS):
        r = lax.broadcasted_iota(jnp.int32, (128, 128), 0)
        pick[:, n * 128 : (n + 1) * 128] = jnp.where((r == n) | (r == n + 2 * NS), 1.0, 0.0).astype(BF16)
    for s in range(SEQS):
        lowp[s, :, RANK:] = jnp.zeros((TOK, LOWW - RANK), BF16)

    half = pl.ds(pl.multiple_of(core * HALF, HALF), HALF)
    other = pl.ds(pl.multiple_of((1 - core) * HALF, HALF), HALF)
    mine = pl.ds(pl.multiple_of(core * HALF + y * OWN, OWN), OWN)

    def share(k):
        return pl.ds(pl.multiple_of(lax.rem(y + k, N_Y) * OWN, OWN), OWN)

    def lsib_copy(s):
        return remote(lowp.at[s, other], lows.at[s], lsib_sem.at[s], sib)

    def low_copy(s, k):
        return remote(lows.at[s, share(k)], lowr.at[s, k - 1], low_sem.at[s, k - 1], at_y(k))

    def nrm_copy(s, k):
        return remote(lown.at[s, mine], lown.at[s, mine], nrm_sem.at[s, k - 1], at_y(k))

    def nsib_copy(s):
        return remote(lown.at[s, half], lown.at[s, half], nsib_sem.at[s], sib)

    def exx_copy(s, k):
        return remote(exx.at[s, x], exx.at[s, x], exx_sem.at[s, k - 1], at_x(k))

    def exz_copy(s, k):
        return remote(exz.at[s, z], exz.at[s, z], exz_sem.at[s, k - 1], at_z(k))

    def low_partial(s):
        conv_block(s, 0)
        rows = act[s * TOK : (s + 1) * TOK, :]
        lowp[s, :, 0:RANK] = jnp.dot(rows, xdt_ref[...], preferred_element_type=F32).astype(BF16)
        lowp[s, :, RANK : RANK + 2 * NS] = lax.dot_general(
            rows, xbc_ref[...], (((1,), (1,)), ((), ())), preferred_element_type=F32
        ).astype(BF16)
        lsib_copy(s).start()

    def low_pair(s):
        lsib_copy(s).wait_recv()
        lows[s] = (lows[s].astype(F32) + lowp[s, half, :].astype(F32)).astype(BF16)
        for k in (2, 1, 3):
            low_copy(s, k).start()

    def normalise(s):
        total = lows[s, share(0), :].astype(F32)
        for k in range(1, N_Y):
            low_copy(s, k).wait_recv()
        for k in range(1, N_Y):
            total = total + lowr[s, k - 1].astype(F32)
        low = total[:, :RANK]
        scale = lax.rsqrt(jnp.mean(low * low, axis=-1, keepdims=True) + 1e-6)
        lown[s, mine, 0:RANK] = (low * scale).astype(BF16)
        bc = total[:, RANK:]
        high = bc.astype(BF16).astype(F32)
        lown[s, mine, RANK:] = (high + pltpu.roll(bc - high, 2 * NS, 1)).astype(BF16)
        for k in (2, 1, 3):
            nrm_copy(s, k).start()

    def low_forward(s):
        for k in range(1, N_Y):
            nrm_copy(s, k).wait_recv()
        nsib_copy(s).start()

    def steps(s):
        nsib_copy(s).wait_recv()
        if s == 0:
            dtw_load.wait()
        pre[...] = jnp.dot(lown[s, :, 0:RANK], dtw_ref[...], preferred_element_type=F32)

        @pl.loop(0, TOK // 16)
        def _(b):
            r = pl.multiple_of(b * 16, 16)
            v = pre[pl.ds(r, 16), :] + dtb_ref[...]
            dt = jnp.maximum(v, 0.0) + jnp.log1p(jnp.exp(-jnp.abs(v)))
            for h in range(2):
                base = pl.multiple_of((s * (TOK // 8) + b * 2 + h) * 64, 64)
                for c in range(NG):
                    dtg[pl.ds(base + c * 8, 8), :] = dt[h * 8 : h * 8 + 8, c * 128 : (c + 1) * 128]

        maps = lown[s, :, RANK:]
        for p in range(2 * NS // 8):
            wide = jnp.dot(maps, pick[:, p * 1024 : (p + 1) * 1024], preferred_element_type=F32)
            for i in range(8):
                at = (p * 8 + i) * ROWS + s * TOK
                splat[at : at + TOK, :] = wide[:, i * 128 : (i + 1) * 128]

    def put_states(dst, s, i, states, elapsed):
        for m in range(NS // 2):
            dst[s, i, m * 16 : (m + 1) * 16, :] = jnp.concatenate(states[2 * m : 2 * m + 2], axis=0).astype(BF16)
        high = elapsed.astype(BF16).astype(F32)
        dst[s, i, NS * 8 :, :] = jnp.concatenate([high, elapsed - high], axis=0).astype(BF16)

    def get_elapsed(src, s, i):
        parts = src[s, i, NS * 8 :, :].astype(F32)
        return parts[0:8] + parts[8:16]

    def first_pass(s):
        rates = [rate_t[n] for n in range(NS)]

        def block(b, carry):
            h, elapsed = list(carry[0]), carry[1]
            base = pl.multiple_of((s * (TOK // 8) + b) * 64, 64)
            for i in range(8):
                dt = dtg[pl.ds(base + i, 8, stride=8), :]
                u = dt * xg[pl.ds(base + i, 8, stride=8), :]
                elapsed = elapsed + dt
                tok = s * TOK + b * 8 + i
                for n in range(NS):
                    h[n] = jnp.exp2(rates[n] * dt) * h[n] + splat[pl.ds(n * ROWS + tok, 1), :] * u
            return (tuple(h), elapsed)

        zero = jnp.zeros((8, 128), F32)
        h, elapsed = lax.fori_loop(0, TOK // 8, block, ((zero,) * NS, zero))
        put_states(exx, s, x, h, elapsed)
        for k in (2, 1, 3):
            exx_copy(s, k).start()

    def along_x(s):
        for k in range(1, N_X):
            exx_copy(s, k).wait_recv()
        spans = [get_elapsed(exx, s, i) for i in range(N_X)]
        totals = []
        for m in range(NS // 2):
            pairs = [exx[s, i, m * 16 : (m + 1) * 16, :].astype(F32) for i in range(N_X)]
            for h in range(2):
                n = 2 * m + h
                state = pairs[0][h * 8 : h * 8 + 8]
                kept = jnp.where(x == 1, state, jnp.zeros_like(state))
                for i in range(1, N_X):
                    state = jnp.exp2(rate_t[n] * spans[i]) * state + pairs[i][h * 8 : h * 8 + 8]
                    if i < N_X - 1:
                        kept = jnp.where(x == i + 1, state, kept)
                before[s, n] = kept
                totals.append(state)
        span = spans[0]
        kept = jnp.where(x == 1, span, jnp.zeros_like(span))
        for i in range(1, N_X):
            span = span + spans[i]
            if i < N_X - 1:
                kept = jnp.where(x == i + 1, span, kept)
        since[s] = kept
        put_states(exz, s, z, totals, span)
        for k in (2, 1, 3):
            exz_copy(s, k).start()

    def along_z(s):
        for k in range(1, N_Z):
            exz_copy(s, k).wait_recv()
        spans = [get_elapsed(exz, s, i) for i in range(N_Z - 1)]
        last_span = since[s]
        for m in range(NS // 2):
            pairs = [exz[s, i, m * 16 : (m + 1) * 16, :].astype(F32) for i in range(N_Z - 1)]
            for h in range(2):
                n = 2 * m + h
                rate = rate_t[n]
                state = init_t[s, n]
                for i in range(N_Z - 1):
                    later = jnp.exp2(rate * spans[i]) * state + pairs[i][h * 8 : h * 8 + 8]
                    state = jnp.where(i < z, later, state)
                ent[s, n] = jnp.exp2(rate * last_span) * state + before[s, n]

    def second_pass(s):
        rates = [rate_t[n] for n in range(NS)]
        skip = skip_ref[...]

        def block(b, h):
            h = list(h)
            base = pl.multiple_of((s * (TOK // 8) + b) * 64, 64)
            for i in range(8):
                dt = dtg[pl.ds(base + i, 8, stride=8), :]
                v = xg[pl.ds(base + i, 8, stride=8), :]
                u = dt * v
                tok = s * TOK + b * 8 + i
                total = skip * v
                for n in range(NS):
                    h[n] = jnp.exp2(rates[n] * dt) * h[n] + splat[pl.ds(n * ROWS + tok, 1), :] * u
                    total = total + splat[pl.ds((NS + n) * ROWS + tok, 1), :] * h[n]
                xg[pl.ds(base + i, 8, stride=8), :] = total
            return tuple(h)

        h = lax.fori_loop(0, TOK // 8, block, tuple(ent[s, n] for n in range(NS)))
        for nb in range(NS // 8):
            for i in range(8):
                flip[pl.ds(i, 8, stride=8), :] = h[nb * 8 + i]
            for c in range(NG):
                st_ref[0, s, nb * 8 : nb * 8 + 8, c * 128 : (c + 1) * 128] = flip[c * 8 : (c + 1) * 8, :]

    def gate(s):
        @pl.loop(0, TOK // 16)
        def _(b):
            r = pl.multiple_of(b * 16, 16)
            v = z_ref[s, pl.ds(r, 16), :].astype(F32)
            sz = v / (1.0 + jnp.exp(-v))
            base = pl.multiple_of((s * (TOK // 8) + b * 2) * 64, 64)
            for c in range(NG):
                scanned = jnp.concatenate(
                    [xg[pl.ds(base + c * 8, 8), :], xg[pl.ds(base + 64 + c * 8, 8), :]], axis=0
                )
                act[pl.ds(pl.multiple_of(s * TOK + r, 16), 16), c * 128 : (c + 1) * 128] = (
                    scanned * sz[:, c * 128 : (c + 1) * 128]
                ).astype(BF16)

    def product(s, j, who):
        dest = lax.rem(y + j, N_Y) * 2 + who
        cols = pl.ds(pl.multiple_of(dest * CH, CH), CH)
        return jnp.dot(act[s * TOK : (s + 1) * TOK, :], w_ref[:, cols], preferred_element_type=F32)

    lo, hi = pl.ds(0, HALF), pl.ds(HALF, HALF)

    def sib_copy(s, j):
        return remote(snd.at[s, j], rcv.at[s, j], sib_sem.at[s, j], sib)

    def opp_up(s):
        return remote(rcv.at[s, 2, lo], opp.at[s, 0], opp_sem.at[s, 0], up)

    def opp_down(s):
        return remote(rcv.at[s, 2, hi], opp.at[s, 1], opp_sem.at[s, 1], down)

    def own_up(s):
        return remote(rcv.at[s, 1, hi], fin.at[s, 0, hi], fin_sem.at[s, 0], up)

    def own_down(s):
        return remote(rcv.at[s, 3, lo], fin.at[s, 1, lo], fin_sem.at[s, 1], down)

    def fwd_up(s):
        return remote(rcv.at[s, 1, lo], fin.at[s, 0, lo], fin_sem.at[s, 2], up)

    def fwd_down(s):
        return remote(rcv.at[s, 3, hi], fin.at[s, 1, hi], fin_sem.at[s, 3], down)

    def for_sibling(s, j):
        snd[s, j] = product(s, j, 1 - core).astype(BF16)
        sib_copy(s, j).start()

    def for_chip(s, j):
        part = product(s, j, core)
        sib_copy(s, j).wait_recv()
        rcv[s, j] = (part + rcv[s, j].astype(F32)).astype(BF16)
        if j == 2:
            opp_up(s).start()
            opp_down(s).start()
        if j == 1:
            own_up(s).start()
        if j == 3:
            own_down(s).start()

    def forward(s):
        for d in range(2):
            (opp_up(s) if d == 0 else opp_down(s)).wait_recv()
            j, r0 = (1, 0) if d == 0 else (3, HALF)

            @pl.loop(0, HALF // 16)
            def _(b):
                r = pl.multiple_of(b * 16, 16)
                part = rcv[s, j, pl.ds(r0 + r, 16), :].astype(F32)
                rcv[s, j, pl.ds(r0 + r, 16), :] = (part + opp[s, d, pl.ds(r, 16), :].astype(F32)).astype(BF16)

            (fwd_up(s) if d == 0 else fwd_down(s)).start()

    def finish(s):
        for c in (own_up(s), own_down(s), fwd_up(s), fwd_down(s)):
            c.wait_recv()

        @pl.loop(0, TOK // 16)
        def _(b):
            r = pl.ds(pl.multiple_of(b * 16, 16), 16)
            total = res_ref[s, r, :].astype(F32) + rcv[s, 0, r, :].astype(F32)
            total = total + fin[s, 0, r, :].astype(F32) + fin[s, 1, r, :].astype(F32)
            out_ref[s, r, :] = total.astype(BF16)

    def project(s):
        along_z(s)
        second_pass(s)
        if s == 0:
            z_load.wait()
        gate(s)
        if s == 0:
            w_load.wait()
        else:
            forward(s - 1)
        for_sibling(s, 2)
        for_sibling(s, 1)
        for_chip(s, 2)
        for_sibling(s, 3)
        for_chip(s, 1)
        for_sibling(s, 0)
        for_chip(s, 3)
        for_chip(s, 0)
        if s == 1:
            res_load.wait()
        if s > 1:
            finish(s - 2)

    rim.wait()
    for s in range(SEQS):
        part = rim_in[...].astype(F32)[(s // 2) * 8 : (s // 2) * 8 + 8, :]
        joined[s, 0:8, :] = pltpu.roll(part, 4, 0) if s % 2 == 0 else part

    @pl.when(q == 0)
    def _():
        for s in range(SEQS):
            joined[s, 5:8, :] = tail_ref[:, s, :].astype(F32)

    xdt_load.wait()
    for s in range(SEQS):
        low_partial(s)
        if s > 0:
            low_pair(s - 1)
    low_pair(SEQS - 1)
    for s in range(SEQS):
        normalise(s)
    low_forward(0)
    low_forward(1)
    steps(0)
    first_pass(0)
    low_forward(2)
    steps(1)
    first_pass(1)
    low_forward(3)
    along_x(0)
    steps(2)
    first_pass(2)
    along_x(1)
    project(0)
    steps(3)
    first_pass(3)
    along_x(2)
    project(1)
    along_x(3)
    project(2)
    project(3)
    forward(3)
    finish(2)
    finish(3)

    for s in range(SEQS):
        lsib_copy(s).wait_send()
        nsib_copy(s).wait_send()
        for k in range(1, N_Y):
            low_copy(s, k).wait_send()
            nrm_copy(s, k).wait_send()
            exx_copy(s, k).wait_send()
            exz_copy(s, k).wait_send()
        for j in range(N_Y):
            sib_copy(s, j).wait_send()
        for c in (opp_up(s), opp_down(s), own_up(s), own_down(s), fwd_up(s), fwd_down(s)):
            c.wait_send()


def place_kernel(out_src, st_src, out_dst, st_dst, out_buf, st_buf, sem):
    arrive, leave = [], []
    for s in range(SEQS):
        arrive.append(pltpu.make_async_copy(out_src.at[s], out_buf.at[s], sem.at[0, s]))
        leave.append(pltpu.make_async_copy(out_buf.at[s], out_dst.at[s], sem.at[1, s]))
    arrive.append(pltpu.make_async_copy(st_src, st_buf, sem.at[0, SEQS]))
    leave.append(pltpu.make_async_copy(st_buf, st_dst, sem.at[1, SEQS]))
    for c in arrive:
        c.start()
    for a, c in zip(arrive, leave):
        a.wait()
        c.start()
    for c in leave:
        c.wait()


def place(out, st):
    anym = pl.BlockSpec(memory_space=pl.ANY)
    return pl.pallas_call(
        place_kernel,
        out_shape=(jax.ShapeDtypeStruct(out.shape, out.dtype), jax.ShapeDtypeStruct(st.shape, st.dtype)),
        in_specs=[anym, anym],
        out_specs=(anym, anym),
        scratch_shapes=[
            pltpu.VMEM(out.shape, out.dtype),
            pltpu.VMEM(st.shape, st.dtype),
            pltpu.SemaphoreType.DMA((2, SEQS + 1)),
        ],
    )(out, st)


def body(
    inner_x,
    inner_z,
    conv_tail,
    conv_weight,
    conv_bias,
    xproj_dt,
    xproj_bc,
    dt_weight,
    dt_bias,
    decay_log,
    skip_gain,
    out_weight,
    residual,
    init_state,
):
    vmem = pl.BlockSpec(memory_space=pltpu.VMEM)
    anym = pl.BlockSpec(memory_space=pl.ANY)
    dma = pltpu.SemaphoreType.DMA
    scratch = [
        pltpu.VMEM((SEQS, TOK, CH), BF16),
        pltpu.VMEM((CH, RANK), BF16),
        pltpu.VMEM((SEQS, NS, CH), F32),
        pltpu.VMEM((RANK, CH), BF16),
        pltpu.VMEM((SEQS, TOK, CH), BF16),
        pltpu.VMEM((CH, N_TP * CH), BF16),
        pltpu.VMEM((SEQS, TOK, CH), BF16),
        pltpu.VMEM((16, CH), BF16),
        pltpu.VMEM((16, CH), BF16),
        pltpu.VMEM((SEQS, TOK + 8, CH), F32),
        pltpu.VMEM((ROWS, CH), BF16),
        pltpu.VMEM((ROWS * 8, 128), F32),
        pltpu.VMEM((ROWS * 8, 128), F32),
        pltpu.VMEM((2 * NS * ROWS, 128), F32),
        pltpu.VMEM((128, 2 * NS * 128), BF16),
        pltpu.VMEM((TOK, CH), F32),
        pltpu.VMEM((NS, 8, 128), F32),
        pltpu.VMEM((SEQS, NS, 8, 128), F32),
        pltpu.VMEM((64, 128), F32),
        pltpu.VMEM((SEQS, TOK, LOWW), BF16),
        pltpu.VMEM((SEQS, HALF, LOWW), BF16),
        pltpu.VMEM((SEQS, N_Y - 1, OWN, LOWW), BF16),
        pltpu.VMEM((SEQS, TOK, LOWW), BF16),
        pltpu.VMEM((SEQS, N_X, EXROWS, 128), BF16),
        pltpu.VMEM((SEQS, N_Z, EXROWS, 128), BF16),
        pltpu.VMEM((SEQS, NS, 8, 128), F32),
        pltpu.VMEM((SEQS, 8, 128), F32),
        pltpu.VMEM((SEQS, NS, 8, 128), F32),
        pltpu.VMEM((SEQS, N_Y, TOK, CH), BF16),
        pltpu.VMEM((SEQS, N_Y, TOK, CH), BF16),
        pltpu.VMEM((SEQS, 2, HALF, CH), BF16),
        pltpu.VMEM((SEQS, 2, TOK, CH), BF16),
        dma((7,)),
        dma((2,)),
        dma((SEQS, 2)),
        dma((SEQS, N_Y - 1, 2)),
        dma((SEQS, N_Y - 1, 2)),
        dma((SEQS, 2)),
        dma((SEQS, N_X - 1, 2)),
        dma((SEQS, N_Z - 1, 2)),
        dma((SEQS, N_Y, 2)),
        dma((SEQS, 2, 2)),
        dma((SEQS, 4, 2)),
    ]
    out, st = pl.pallas_call(
        mix_kernel,
        out_shape=(
            jax.ShapeDtypeStruct((SEQS, TOK, CH), BF16),
            jax.ShapeDtypeStruct((1, SEQS, NS, CH), F32),
        ),
        in_specs=[vmem] * 7 + [anym] * 7,
        out_specs=(vmem, vmem),
        scratch_shapes=scratch,
        compiler_params=pltpu.CompilerParams(
            collective_id=0, has_side_effects=True, vmem_limit_bytes=62 * 1024 * 1024
        ),
    )(
        jnp.transpose(conv_tail, (1, 0, 2)),
        conv_weight,
        conv_bias.reshape(1, CH),
        xproj_bc.T,
        dt_bias.reshape(1, CH),
        decay_log,
        skip_gain.reshape(8, 128),
        inner_x,
        xproj_dt,
        init_state,
        dt_weight,
        inner_z,
        out_weight,
        residual,
    )
    return place(out, st)


def solution(mesh):
    in_specs = (
        P(None, "seq", "tp"),
        P(None, "seq", "tp"),
        P(None, None, "tp"),
        P(None, "tp"),
        P("tp"),
        P("tp", None),
        P("tp", None),
        P(None, "tp"),
        P("tp"),
        P(None, "tp"),
        P("tp"),
        P("tp", None),
        P(None, "seq", "tp"),
        P(None, None, "tp"),
    )
    out_specs = (P(None, "seq", "tp"), P("seq", None, None, "tp"))
    return jax.shard_map(body, mesh=mesh, in_specs=in_specs, out_specs=out_specs, check_vma=False)
```

time: 112 us -> 82.7 us (0.74)
  Pallas kernels: 104 us -> 81.7 us
  local copies, waits for them, and re-layouts: 6.98 us -> 0 us
    pallas_call x1, Pallas kernels: 104 us -> 79.6 us  [body(): pl.pallas_call(mix_kernel, out_shape=(jax.ShapeDtypeStruct((SEQS, TOK, CH...]
    unnamed x4 -> x0, local copies, waits for them, and re-layouts: 6.98 us -> none
    pallas_call x0 -> x1, Pallas kernels: none -> 2.08 us  [place(): pl.pallas_call(place_kernel, out_shape=(jax.ShapeDtypeStruct(out.shape, o...]
where the time goes in v2:
time: 82.7 us; the launch traced here: 82.5 us
  Pallas kernels  81.7 us (99%)
    pallas_call x1, Pallas kernels, body(): pl.pallas_call(mix_kernel, out_shape=(jax.ShapeDtypeStruct((SEQS, TOK, CH...  79.6 us
    pallas_call x1, Pallas kernels, place(): pl.pallas_call(place_kernel, out_shape=(jax.ShapeDtypeStruct(out.shape, o...  2.08 us

profile of v2, /device:TPU:1, one launch (start us, length us, event | category | flops | bytes accessed | tf_op | source)
XLA Modules:
  0.0 82.5 jit_solution(14251472561030203887)
XLA Ops:
  0.6 79.6 %shard_map.149 = (bf16[4,128,1024]{2,1,0:T(8,128)(2,1)}, f32[1,4,16,1024]{3,2,1,0:T(8,128)}) custom-call(bf16[3,4,1024]{2,1,0:T(4,128)(2,1)} %bitcast.6, f32[4,1024]{1,0:T(4,128)} %cw_ref.1, f32[1,1024]{1,0:T(1,128)} %bitcast.7, bf16[32,1024]{1,0:T(8,128)(2,1)} %bitcast.5, f32[1,1024]{1,0:T(1,128)} %bitcast.8, f32[16,1024]{1,0:T(8,128)} %decay_ref.1, ...), custom_call_target="tpu_custom_call" | custom-call | tf_op jit(solution)/shard_map/pallas_call | solution.py:639
  80.3 2.1 %shard_map.150 = (bf16[4,128,1024]{2,1,0:T(8,128)(2,1)}, f32[1,4,16,1024]{3,2,1,0:T(8,128)}) custom-call(bf16[4,128,1024]{2,1,0:T(8,128)(2,1)} %get-tuple-element.4.out_src, f32[1,4,16,1024]{3,2,1,0:T(8,128)} %get-tuple-element.5.st_src), custom_call_target="tpu_custom_call" | custom-call | tf_op jit(solution)/shard_map/pallas_call | solution.py:562

commit v3 on v2

--- a/solution.py
+++ b/solution.py
@@ -29,13 +29,13 @@
 
 
 def mix_kernel(
-    tail_ref,
-    cw_ref,
-    cb_ref,
-    xbc_ref,
-    dtb_ref,
-    decay_ref,
-    skip_ref,
+    tail_hbm,
+    cw_hbm,
+    cb_hbm,
+    xbc_hbm,
+    dtb_hbm,
+    decay_hbm,
+    skip_hbm,
     x_hbm,
     xdt_hbm,
     init_hbm,
@@ -45,6 +45,13 @@
     res_hbm,
     out_ref,
     st_ref,
+    tail_ref,
+    cw_ref,
+    cb_ref,
+    xbc_ref,
+    dtb_ref,
+    decay_ref,
+    skip_ref,
     x_ref,
     xdt_ref,
     init_ref,
@@ -73,8 +80,8 @@
     before,
     since,
     ent,
-    snd,
-    rcv,
+    both,
+    part,
     opp,
     fin,
     load_sem,
@@ -85,7 +92,9 @@
     nsib_sem,
     exx_sem,
     exz_sem,
-    sib_sem,
+    wown_sem,
+    wsib_sem,
+    both_sem,
     opp_sem,
     fin_sem,
 ):
@@ -122,23 +131,45 @@
         for i, (src, dst) in enumerate(
             (
                 (x_hbm, x_ref),
+                (cw_hbm, cw_ref),
+                (cb_hbm, cb_ref),
+                (tail_hbm, tail_ref),
                 (xdt_hbm, xdt_ref),
+                (xbc_hbm, xbc_ref),
+                (decay_hbm, decay_ref),
+                (dtb_hbm, dtb_ref),
+                (skip_hbm, skip_ref),
+                (dtw_hbm, dtw_ref),
                 (init_hbm, init_ref),
-                (dtw_hbm, dtw_ref),
-                (w_hbm, w_ref),
                 (z_hbm, z_ref),
                 (res_hbm, res_ref),
             )
         )
     ]
-    x_load, xdt_load, init_load, dtw_load, w_load, z_load, res_load = loads
-    x_load.start()
+
+    own_rows = pl.ds(pl.multiple_of(core * CH, CH), CH)
+
+    def w_block(j):
+        return pl.ds(pl.multiple_of(lax.rem(y + j, N_Y) * CH, CH), CH)
+
+    def w_source(j, who):
+        return w_hbm.at[:, pl.ds(pl.multiple_of((lax.rem(y + j, N_Y) * 2 + who) * CH, CH), CH)]
+
+    def w_own(j):
+        return pltpu.make_async_copy(w_source(j, core), w_ref.at[own_rows, w_block(j)], wown_sem.at[j])
+
+    def w_give(j):
+        return remote(w_source(j, 1 - core), w_ref.at[own_rows, w_block(j)], wsib_sem.at[j], sib)
+
+    loads[0].start()
     for dev in peers:
         pl.semaphore_signal(barrier, inc=1, device_id=dev, device_id_type=MESH)
     for c in loads[1:]:
         c.start()
-
-    x_load.wait()
+    for j in (2, 1, 3, 0):
+        w_own(j).start()
+
+    loads[0].wait()
     row8 = lax.broadcasted_iota(jnp.int32, (8, CH), 0)
     last = [x_ref[s, TOK - 16 : TOK, :].astype(F32)[8:16, :] for s in range(SEQS)]
     packed = [jnp.where(row8 < 4, pltpu.roll(last[s], 4, 0), last[s + 1]) for s in (0, 2)]
@@ -147,6 +178,7 @@
     pl.semaphore_wait(barrier, len(peers))
     rim = remote(rim_out, rim_in, rim_sem, after)
     rim.start()
+    w_give(2).start()
 
     def conv_block(s, b):
         r = pl.multiple_of(b * 16, 16)
@@ -162,6 +194,9 @@
             for c in range(NG):
                 xg[pl.ds(base + c * 8, 8), :] = wide[h * 8 : h * 8 + 8, c * 128 : (c + 1) * 128]
 
+    loads[1].wait()
+    loads[2].wait()
+
     @pl.loop(0, SEQS)
     def _(s):
         @pl.loop(0, TOK // 16)
@@ -173,25 +208,6 @@
         def _(b):
             conv_block(s, b)
 
-    for nb in range(NS // 8):
-        for c in range(NG):
-            flip[c * 8 : (c + 1) * 8, :] = -jnp.exp(decay_ref[nb * 8 : nb * 8 + 8, c * 128 : (c + 1) * 128]) * LOG2E
-        for i in range(8):
-            rate_t[nb * 8 + i] = flip[pl.ds(i, 8, stride=8), :]
-
-    init_load.wait()
-
-    @pl.loop(0, SEQS)
-    def _(s):
-        for nb in range(NS // 8):
-            for c in range(NG):
-                flip[c * 8 : (c + 1) * 8, :] = init_ref[s, nb * 8 : nb * 8 + 8, c * 128 : (c + 1) * 128]
-            for i in range(8):
-                init_t[s, nb * 8 + i] = flip[pl.ds(i, 8, stride=8), :]
-
-    for n in range(2 * NS):
-        r = lax.broadcasted_iota(jnp.int32, (128, 128), 0)
-        pick[:, n * 128 : (n + 1) * 128] = jnp.where((r == n) | (r == n + 2 * NS), 1.0, 0.0).astype(BF16)
     for s in range(SEQS):
         lowp[s, :, RANK:] = jnp.zeros((TOK, LOWW - RANK), BF16)
 
@@ -258,7 +274,7 @@
     def steps(s):
         nsib_copy(s).wait_recv()
         if s == 0:
-            dtw_load.wait()
+            loads[9].wait()
         pre[...] = jnp.dot(lown[s, :, 0:RANK], dtw_ref[...], preferred_element_type=F32)
 
         @pl.loop(0, TOK // 16)
@@ -390,46 +406,38 @@
                 scanned = jnp.concatenate(
                     [xg[pl.ds(base + c * 8, 8), :], xg[pl.ds(base + 64 + c * 8, 8), :]], axis=0
                 )
-                act[pl.ds(pl.multiple_of(s * TOK + r, 16), 16), c * 128 : (c + 1) * 128] = (
+                both[s, pl.ds(r, 16), pl.ds(pl.multiple_of(core * CH + c * 128, 128), 128)] = (
                     scanned * sz[:, c * 128 : (c + 1) * 128]
                 ).astype(BF16)
 
-    def product(s, j, who):
-        dest = lax.rem(y + j, N_Y) * 2 + who
-        cols = pl.ds(pl.multiple_of(dest * CH, CH), CH)
-        return jnp.dot(act[s * TOK : (s + 1) * TOK, :], w_ref[:, cols], preferred_element_type=F32)
-
     lo, hi = pl.ds(0, HALF), pl.ds(HALF, HALF)
 
-    def sib_copy(s, j):
-        return remote(snd.at[s, j], rcv.at[s, j], sib_sem.at[s, j], sib)
+    def both_copy(s):
+        return remote(both.at[s, :, own_rows], both.at[s, :, own_rows], both_sem.at[s], sib)
 
     def opp_up(s):
-        return remote(rcv.at[s, 2, lo], opp.at[s, 0], opp_sem.at[s, 0], up)
+        return remote(part.at[s, 2, lo], opp.at[s, 0], opp_sem.at[s, 0], up)
 
     def opp_down(s):
-        return remote(rcv.at[s, 2, hi], opp.at[s, 1], opp_sem.at[s, 1], down)
+        return remote(part.at[s, 2, hi], opp.at[s, 1], opp_sem.at[s, 1], down)
 
     def own_up(s):
-        return remote(rcv.at[s, 1, hi], fin.at[s, 0, hi], fin_sem.at[s, 0], up)
+        return remote(part.at[s, 1, hi], fin.at[s, 0, hi], fin_sem.at[s, 0], up)
 
     def own_down(s):
-        return remote(rcv.at[s, 3, lo], fin.at[s, 1, lo], fin_sem.at[s, 1], down)
+        return remote(part.at[s, 3, lo], fin.at[s, 1, lo], fin_sem.at[s, 1], down)
 
     def fwd_up(s):
-        return remote(rcv.at[s, 1, lo], fin.at[s, 0, lo], fin_sem.at[s, 2], up)
+        return remote(part.at[s, 1, lo], fin.at[s, 0, lo], fin_sem.at[s, 2], up)
 
     def fwd_down(s):
-        return remote(rcv.at[s, 3, hi], fin.at[s, 1, hi], fin_sem.at[s, 3], down)
-
-    def for_sibling(s, j):
-        snd[s, j] = product(s, j, 1 - core).astype(BF16)
-        sib_copy(s, j).start()
+        return remote(part.at[s, 3, hi], fin.at[s, 1, hi], fin_sem.at[s, 3], down)
 
     def for_chip(s, j):
-        part = product(s, j, core)
-        sib_copy(s, j).wait_recv()
-        rcv[s, j] = (part + rcv[s, j].astype(F32)).astype(BF16)
+        if s == 0:
+            w_own(j).wait()
+            w_give(j).wait_recv()
+        part[s, j] = jnp.dot(both[s], w_ref[:, w_block(j)], preferred_element_type=F32).astype(BF16)
         if j == 2:
             opp_up(s).start()
             opp_down(s).start()
@@ -446,8 +454,8 @@
             @pl.loop(0, HALF // 16)
             def _(b):
                 r = pl.multiple_of(b * 16, 16)
-                part = rcv[s, j, pl.ds(r0 + r, 16), :].astype(F32)
-                rcv[s, j, pl.ds(r0 + r, 16), :] = (part + opp[s, d, pl.ds(r, 16), :].astype(F32)).astype(BF16)
+                here = part[s, j, pl.ds(r0 + r, 16), :].astype(F32)
+                part[s, j, pl.ds(r0 + r, 16), :] = (here + opp[s, d, pl.ds(r, 16), :].astype(F32)).astype(BF16)
 
             (fwd_up(s) if d == 0 else fwd_down(s)).start()
 
@@ -458,7 +466,7 @@
         @pl.loop(0, TOK // 16)
         def _(b):
             r = pl.ds(pl.multiple_of(b * 16, 16), 16)
-            total = res_ref[s, r, :].astype(F32) + rcv[s, 0, r, :].astype(F32)
+            total = res_ref[s, r, :].astype(F32) + part[s, 0, r, :].astype(F32)
             total = total + fin[s, 0, r, :].astype(F32) + fin[s, 1, r, :].astype(F32)
             out_ref[s, r, :] = total.astype(BF16)
 
@@ -466,47 +474,67 @@
         along_z(s)
         second_pass(s)
         if s == 0:
-            z_load.wait()
+            loads[11].wait()
         gate(s)
-        if s == 0:
-            w_load.wait()
-        else:
-            forward(s - 1)
-        for_sibling(s, 2)
-        for_sibling(s, 1)
-        for_chip(s, 2)
-        for_sibling(s, 3)
-        for_chip(s, 1)
-        for_sibling(s, 0)
-        for_chip(s, 3)
-        for_chip(s, 0)
-        if s == 1:
-            res_load.wait()
-        if s > 1:
-            finish(s - 2)
-
+        both_copy(s).start()
+
+    def combine(s):
+        both_copy(s).wait_recv()
+        for j in (2, 1, 3, 0):
+            for_chip(s, j)
+
+    loads[3].wait()
     rim.wait()
     for s in range(SEQS):
-        part = rim_in[...].astype(F32)[(s // 2) * 8 : (s // 2) * 8 + 8, :]
-        joined[s, 0:8, :] = pltpu.roll(part, 4, 0) if s % 2 == 0 else part
+        rows = rim_in[...].astype(F32)[(s // 2) * 8 : (s // 2) * 8 + 8, :]
+        joined[s, 0:8, :] = pltpu.roll(rows, 4, 0) if s % 2 == 0 else rows
 
     @pl.when(q == 0)
     def _():
         for s in range(SEQS):
             joined[s, 5:8, :] = tail_ref[:, s, :].astype(F32)
 
-    xdt_load.wait()
+    loads[4].wait()
+    loads[5].wait()
     for s in range(SEQS):
         low_partial(s)
         if s > 0:
             low_pair(s - 1)
     low_pair(SEQS - 1)
+    w_give(1).start()
     for s in range(SEQS):
         normalise(s)
+
+    for i in (6, 7, 8):
+        loads[i].wait()
+
+    for nb in range(NS // 8):
+        for c in range(NG):
+            flip[c * 8 : (c + 1) * 8, :] = -jnp.exp(decay_ref[nb * 8 : nb * 8 + 8, c * 128 : (c + 1) * 128]) * LOG2E
+        for i in range(8):
+            rate_t[nb * 8 + i] = flip[pl.ds(i, 8, stride=8), :]
+
+    for n in range(2 * NS):
+        r = lax.broadcasted_iota(jnp.int32, (128, 128), 0)
+        pick[:, n * 128 : (n + 1) * 128] = jnp.where((r == n) | (r == n + 2 * NS), 1.0, 0.0).astype(BF16)
+
     low_forward(0)
+    w_give(3).start()
     low_forward(1)
     steps(0)
     first_pass(0)
+    w_give(0).start()
+
+    loads[10].wait()
+
+    @pl.loop(0, SEQS)
+    def _(s):
+        for nb in range(NS // 8):
+            for c in range(NG):
+                flip[c * 8 : (c + 1) * 8, :] = init_ref[s, nb * 8 : nb * 8 + 8, c * 128 : (c + 1) * 128]
+            for i in range(8):
+                init_t[s, nb * 8 + i] = flip[pl.ds(i, 8, stride=8), :]
+
     low_forward(2)
     steps(1)
     first_pass(1)
@@ -517,16 +545,28 @@
     along_x(1)
     project(0)
     steps(3)
-    first_pass(3)
+    combine(0)
     along_x(2)
     project(1)
+    forward(0)
+    combine(1)
+    first_pass(3)
+    project(2)
+    loads[12].wait()
+    forward(1)
     along_x(3)
-    project(2)
+    combine(2)
+    finish(0)
     project(3)
+    forward(2)
+    combine(3)
+    finish(1)
+    finish(2)
     forward(3)
-    finish(2)
     finish(3)
 
+    for j in range(N_Y):
+        w_give(j).wait_send()
     for s in range(SEQS):
         lsib_copy(s).wait_send()
         nsib_copy(s).wait_send()
@@ -535,41 +575,9 @@
             nrm_copy(s, k).wait_send()
             exx_copy(s, k).wait_send()
             exz_copy(s, k).wait_send()
-        for j in range(N_Y):
-            sib_copy(s, j).wait_send()
+        both_copy(s).wait_send()
         for c in (opp_up(s), opp_down(s), own_up(s), own_down(s), fwd_up(s), fwd_down(s)):
             c.wait_send()
-
-
-def place_kernel(out_src, st_src, out_dst, st_dst, out_buf, st_buf, sem):
-    arrive, leave = [], []
-    for s in range(SEQS):
-        arrive.append(pltpu.make_async_copy(out_src.at[s], out_buf.at[s], sem.at[0, s]))
-        leave.append(pltpu.make_async_copy(out_buf.at[s], out_dst.at[s], sem.at[1, s]))
-    arrive.append(pltpu.make_async_copy(st_src, st_buf, sem.at[0, SEQS]))
-    leave.append(pltpu.make_async_copy(st_buf, st_dst, sem.at[1, SEQS]))
-    for c in arrive:
-        c.start()
-    for a, c in zip(arrive, leave):
-        a.wait()
-        c.start()
-    for c in leave:
-        c.wait()
-
-
-def place(out, st):
-    anym = pl.BlockSpec(memory_space=pl.ANY)
-    return pl.pallas_call(
-        place_kernel,
-        out_shape=(jax.ShapeDtypeStruct(out.shape, out.dtype), jax.ShapeDtypeStruct(st.shape, st.dtype)),
-        in_specs=[anym, anym],
-        out_specs=(anym, anym),
-        scratch_shapes=[
-            pltpu.VMEM(out.shape, out.dtype),
-            pltpu.VMEM(st.shape, st.dtype),
-            pltpu.SemaphoreType.DMA((2, SEQS + 1)),
-        ],
-    )(out, st)
 
 
 def body(
@@ -592,12 +600,19 @@
     anym = pl.BlockSpec(memory_space=pl.ANY)
     dma = pltpu.SemaphoreType.DMA
     scratch = [
+        pltpu.VMEM((3, SEQS, CH), BF16),
+        pltpu.VMEM((4, CH), F32),
+        pltpu.VMEM((1, CH), F32),
+        pltpu.VMEM((2 * NS, CH), BF16),
+        pltpu.VMEM((1, CH), F32),
+        pltpu.VMEM((NS, CH), F32),
+        pltpu.VMEM((8, 128), F32),
         pltpu.VMEM((SEQS, TOK, CH), BF16),
         pltpu.VMEM((CH, RANK), BF16),
         pltpu.VMEM((SEQS, NS, CH), F32),
         pltpu.VMEM((RANK, CH), BF16),
         pltpu.VMEM((SEQS, TOK, CH), BF16),
-        pltpu.VMEM((CH, N_TP * CH), BF16),
+        pltpu.VMEM((2 * CH, N_Y * CH), BF16),
         pltpu.VMEM((SEQS, TOK, CH), BF16),
         pltpu.VMEM((16, CH), BF16),
         pltpu.VMEM((16, CH), BF16),
@@ -620,11 +635,11 @@
         pltpu.VMEM((SEQS, NS, 8, 128), F32),
         pltpu.VMEM((SEQS, 8, 128), F32),
         pltpu.VMEM((SEQS, NS, 8, 128), F32),
-        pltpu.VMEM((SEQS, N_Y, TOK, CH), BF16),
+        pltpu.VMEM((SEQS, TOK, 2 * CH), BF16),
         pltpu.VMEM((SEQS, N_Y, TOK, CH), BF16),
         pltpu.VMEM((SEQS, 2, HALF, CH), BF16),
         pltpu.VMEM((SEQS, 2, TOK, CH), BF16),
-        dma((7,)),
+        dma((13,)),
         dma((2,)),
         dma((SEQS, 2)),
         dma((SEQS, N_Y - 1, 2)),
@@ -632,17 +647,19 @@
         dma((SEQS, 2)),
         dma((SEQS, N_X - 1, 2)),
         dma((SEQS, N_Z - 1, 2)),
-        dma((SEQS, N_Y, 2)),
+        dma((N_Y,)),
+        dma((N_Y, 2)),
+        dma((SEQS, 2)),
         dma((SEQS, 2, 2)),
         dma((SEQS, 4, 2)),
     ]
     out, st = pl.pallas_call(
         mix_kernel,
         out_shape=(
-            jax.ShapeDtypeStruct((SEQS, TOK, CH), BF16),
-            jax.ShapeDtypeStruct((1, SEQS, NS, CH), F32),
+            pltpu.VMEM((SEQS, TOK, CH), BF16),
+            pltpu.VMEM((1, SEQS, NS, CH), F32),
         ),
-        in_specs=[vmem] * 7 + [anym] * 7,
+        in_specs=[anym] * 14,
         out_specs=(vmem, vmem),
         scratch_shapes=scratch,
         compiler_params=pltpu.CompilerParams(
@@ -664,7 +681,7 @@
         out_weight,
         residual,
     )
-    return place(out, st)
+    return out, st
 
 
 def solution(mesh):

time: 82.7 us -> 77 us (0.931)
  Pallas kernels: 81.7 us -> 74.6 us
  local copies, waits for them, and re-layouts: 0 us -> 1.67 us
    pallas_call x2 -> x1, Pallas kernels: 81.7 us -> 74.6 us  [body(): pl.pallas_call(mix_kernel, out_shape=(pltpu.VMEM((SEQS, TOK, CH), BF16),...]
    unnamed x0 -> x2, local copies, waits for them, and re-layouts: none -> 1.67 us
where the time goes in v3:
time: 77 us; the launch traced here: 76.9 us
  Pallas kernels  74.6 us (97%)
  local copies, waits for them, and re-layouts  1.67 us (2%)
    pallas_call x1, Pallas kernels, body(): pl.pallas_call(mix_kernel, out_shape=(pltpu.VMEM((SEQS, TOK, CH), BF16),...  74.6 us
    unnamed x2, local copies, waits for them, and re-layouts  1.67 us

profile of v3, /device:TPU:1, one launch (start us, length us, event | category | flops | bytes accessed | tf_op | source)
XLA Modules:
  0.0 76.9 jit_solution(4097344508028096146)
XLA Ops:
  0.6 74.6 %shard_map.149 = (bf16[4,128,1024]{2,1,0:T(8,128)(2,1)S(1)}, f32[1,4,16,1024]{3,2,1,0:T(8,128)S(1)}) custom-call(bf16[3,4,1024]{2,1,0:T(4,128)(2,1)} %bitcast.6, f32[4,1024]{1,0:T(4,128)} %cw_hbm.1, f32[1,1024]{1,0:T(1,128)} %bitcast.7, bf16[32,1024]{1,0:T(8,128)(2,1)} %bitcast.5, f32[1,1024]{1,0:T(1,128)} %bitcast.8, f32[16,1024]{1,0:T(8,128)} %decay_hbm.1, ...), custom_call_target="tpu_custom_call" | custom-call | tf_op jit(solution)/shard_map/pallas_call | solution.py:656
  75.3 1.0 %copy.18 = bf16[4,128,1024]{2,1,0:T(8,128)(2,1)} copy(bf16[4,128,1024]{2,1,0:T(8,128)(2,1)S(1)} %get-tuple-element.2) | data formatting | bytes 2097152
  76.2 0.7 copy.19

commit v4 on v3

--- a/solution.py
+++ b/solution.py
@@ -124,7 +124,7 @@
         )
 
     barrier = pltpu.get_barrier_semaphore()
-    peers = [after, prior, sib] + [at_y(k) for k in (1, 2, 3)]
+    peers = [prior, sib] + [at_y(k) for k in (1, 2, 3)]
     peers += [at_x(k) for k in (1, 2, 3)] + [at_z(k) for k in (1, 2, 3)]
     loads = [
         pltpu.make_async_copy(src, dst, load_sem.at[i])
@@ -478,9 +478,12 @@
         gate(s)
         both_copy(s).start()
 
-    def combine(s):
+    def far(s):
         both_copy(s).wait_recv()
-        for j in (2, 1, 3, 0):
+        for_chip(s, 2)
+
+    def near(s):
+        for j in (1, 3, 0):
             for_chip(s, j)
 
     loads[3].wait()
@@ -545,24 +548,28 @@
     along_x(1)
     project(0)
     steps(3)
-    combine(0)
+    far(0)
+    near(0)
     along_x(2)
     project(1)
+    first_pass(3)
     forward(0)
-    combine(1)
-    first_pass(3)
+    far(1)
+    near(1)
     project(2)
+    along_x(3)
+    far(2)
+    forward(1)
+    near(2)
     loads[12].wait()
-    forward(1)
-    along_x(3)
-    combine(2)
     finish(0)
     project(3)
+    far(3)
     forward(2)
-    combine(3)
+    near(3)
     finish(1)
+    forward(3)
     finish(2)
-    forward(3)
     finish(3)
 
     for j in range(N_Y):

time: 77 us -> 78.3 us (1.017)
  Pallas kernels: 74.6 us -> 75.9 us
    pallas_call x1, Pallas kernels: 74.6 us -> 75.9 us  [body(): pl.pallas_call(mix_kernel, out_shape=(pltpu.VMEM((SEQS, TOK, CH), BF16),...]
where the time goes in v4:
time: 78.3 us; the launch traced here: 78.2 us
  Pallas kernels  75.9 us (97%)
  local copies, waits for them, and re-layouts  1.67 us (2%)
    pallas_call x1, Pallas kernels, body(): pl.pallas_call(mix_kernel, out_shape=(pltpu.VMEM((SEQS, TOK, CH), BF16),...  75.9 us
    unnamed x2, local copies, waits for them, and re-layouts  1.67 us

profile of v4, /device:TPU:1, one launch (start us, length us, event | category | flops | bytes accessed | tf_op | source)
XLA Modules:
  0.0 78.2 jit_solution(15373333813587269902)
XLA Ops:
  0.6 75.9 %shard_map.149 = (bf16[4,128,1024]{2,1,0:T(8,128)(2,1)S(1)}, f32[1,4,16,1024]{3,2,1,0:T(8,128)S(1)}) custom-call(bf16[3,4,1024]{2,1,0:T(4,128)(2,1)} %bitcast.6, f32[4,1024]{1,0:T(4,128)} %cw_hbm.1, f32[1,1024]{1,0:T(1,128)} %bitcast.7, bf16[32,1024]{1,0:T(8,128)(2,1)} %bitcast.5, f32[1,1024]{1,0:T(1,128)} %bitcast.8, f32[16,1024]{1,0:T(8,128)} %decay_hbm.1, ...), custom_call_target="tpu_custom_call" | custom-call | tf_op jit(solution)/shard_map/pallas_call | solution.py:663
  76.5 1.0 %copy.18 = bf16[4,128,1024]{2,1,0:T(8,128)(2,1)} copy(bf16[4,128,1024]{2,1,0:T(8,128)(2,1)S(1)} %get-tuple-element.2) | data formatting | bytes 2097152
  77.5 0.7 copy.19

commit v5 on v4

--- a/solution.py
+++ b/solution.py
@@ -399,8 +399,7 @@
         @pl.loop(0, TOK // 16)
         def _(b):
             r = pl.multiple_of(b * 16, 16)
-            v = z_ref[s, pl.ds(r, 16), :].astype(F32)
-            sz = v / (1.0 + jnp.exp(-v))
+            sz = joined[s, pl.ds(r + 8, 16), :]
             base = pl.multiple_of((s * (TOK // 8) + b * 2) * 64, 64)
             for c in range(NG):
                 scanned = jnp.concatenate(
@@ -473,8 +472,6 @@
     def project(s):
         along_z(s)
         second_pass(s)
-        if s == 0:
-            loads[11].wait()
         gate(s)
         both_copy(s).start()
 
@@ -521,6 +518,16 @@
         r = lax.broadcasted_iota(jnp.int32, (128, 128), 0)
         pick[:, n * 128 : (n + 1) * 128] = jnp.where((r == n) | (r == n + 2 * NS), 1.0, 0.0).astype(BF16)
 
+    loads[11].wait()
+
+    @pl.loop(0, SEQS)
+    def _(s):
+        @pl.loop(0, TOK // 16)
+        def _(b):
+            r = pl.multiple_of(b * 16, 16)
+            v = z_ref[s, pl.ds(r, 16), :].astype(F32)
+            joined[s, pl.ds(r + 8, 16), :] = v / (1.0 + jnp.exp(-v))
+
     low_forward(0)
     w_give(3).start()
     low_forward(1)
@@ -542,31 +549,31 @@
     steps(1)
     first_pass(1)
     low_forward(3)
+    steps(2)
     along_x(0)
-    steps(2)
     first_pass(2)
     along_x(1)
+    steps(3)
     project(0)
-    steps(3)
+    along_x(2)
+    first_pass(3)
     far(0)
     near(0)
-    along_x(2)
     project(1)
-    first_pass(3)
+    along_x(3)
+    project(2)
     forward(0)
     far(1)
     near(1)
-    project(2)
-    along_x(3)
+    project(3)
     far(2)
+    near(2)
     forward(1)
-    near(2)
+    far(3)
+    near(3)
     loads[12].wait()
     finish(0)
-    project(3)
-    far(3)
     forward(2)
-    near(3)
     finish(1)
     forward(3)
     finish(2)

time: 78.3 us -> 79.7 us (1.018)
  Pallas kernels: 75.9 us -> 77.2 us
    pallas_call x1, Pallas kernels: 75.9 us -> 77.2 us  [body(): pl.pallas_call(mix_kernel, out_shape=(pltpu.VMEM((SEQS, TOK, CH), BF16),...]
where the time goes in v5:
time: 79.7 us; the launch traced here: 79.6 us
  Pallas kernels  77.2 us (97%)
  local copies, waits for them, and re-layouts  1.67 us (2%)
    pallas_call x1, Pallas kernels, body(): pl.pallas_call(mix_kernel, out_shape=(pltpu.VMEM((SEQS, TOK, CH), BF16),...  77.2 us
    unnamed x2, local copies, waits for them, and re-layouts  1.67 us

profile of v5, /device:TPU:1, one launch (start us, length us, event | category | flops | bytes accessed | tf_op | source)
XLA Modules:
  0.0 79.6 jit_solution(11548237261711047899)
XLA Ops:
  0.6 77.2 %shard_map.149 = (bf16[4,128,1024]{2,1,0:T(8,128)(2,1)S(1)}, f32[1,4,16,1024]{3,2,1,0:T(8,128)S(1)}) custom-call(bf16[3,4,1024]{2,1,0:T(4,128)(2,1)} %bitcast.6, f32[4,1024]{1,0:T(4,128)} %cw_hbm.1, f32[1,1024]{1,0:T(1,128)} %bitcast.7, bf16[32,1024]{1,0:T(8,128)(2,1)} %bitcast.5, f32[1,1024]{1,0:T(1,128)} %bitcast.8, f32[16,1024]{1,0:T(8,128)} %decay_hbm.1, ...), custom_call_target="tpu_custom_call" | custom-call | tf_op jit(solution)/shard_map/pallas_call | solution.py:670
  77.9 1.0 %copy.18 = bf16[4,128,1024]{2,1,0:T(8,128)(2,1)} copy(bf16[4,128,1024]{2,1,0:T(8,128)(2,1)S(1)} %get-tuple-element.2) | data formatting | bytes 2097152
  78.9 0.7 copy.19

commit v6 on v3

--- a/solution.py
+++ b/solution.py
@@ -26,6 +26,7 @@
 HALF = TOK // 2
 OWN = HALF // N_Y
 EXROWS = (NS + 2) * 8
+ENDS = (0, SEQS - 1)
 
 
 def mix_kernel(
@@ -124,7 +125,7 @@
         )
 
     barrier = pltpu.get_barrier_semaphore()
-    peers = [after, prior, sib] + [at_y(k) for k in (1, 2, 3)]
+    peers = [prior, sib] + [at_y(k) for k in (1, 2, 3)]
     peers += [at_x(k) for k in (1, 2, 3)] + [at_z(k) for k in (1, 2, 3)]
     loads = [
         pltpu.make_async_copy(src, dst, load_sem.at[i])
@@ -441,9 +442,9 @@
         if j == 2:
             opp_up(s).start()
             opp_down(s).start()
-        if j == 1:
+        if j == 1 and s not in ENDS:
             own_up(s).start()
-        if j == 3:
+        if j == 3 and s not in ENDS:
             own_down(s).start()
 
     def forward(s):
@@ -482,6 +483,11 @@
         both_copy(s).wait_recv()
         for j in (2, 1, 3, 0):
             for_chip(s, j)
+        if s in ENDS:
+            opp_up(s).wait_send()
+            opp_down(s).wait_send()
+            own_up(s).start()
+            own_down(s).start()
 
     loads[3].wait()
     rim.wait()
@@ -552,17 +558,17 @@
     combine(1)
     first_pass(3)
     project(2)
-    loads[12].wait()
     forward(1)
     along_x(3)
     combine(2)
-    finish(0)
     project(3)
     forward(2)
     combine(3)
+    loads[12].wait()
+    finish(0)
     finish(1)
+    forward(3)
     finish(2)
-    forward(3)
     finish(3)
 
     for j in range(N_Y):
@@ -576,7 +582,10 @@
             exx_copy(s, k).wait_send()
             exz_copy(s, k).wait_send()
         both_copy(s).wait_send()
-        for c in (opp_up(s), opp_down(s), own_up(s), own_down(s), fwd_up(s), fwd_down(s)):
+        if s not in ENDS:
+            opp_up(s).wait_send()
+            opp_down(s).wait_send()
+        for c in (own_up(s), own_down(s), fwd_up(s), fwd_down(s)):
             c.wait_send()
 
 

time: 77 us -> 77.7 us (level)
  no operation moved by 1% of the time
where the time goes in v6:
time: 77.7 us; the launch traced here: 77.4 us
  Pallas kernels  75 us (97%)
  local copies, waits for them, and re-layouts  1.67 us (2%)
    pallas_call x1, Pallas kernels, body(): pl.pallas_call(mix_kernel, out_shape=(pltpu.VMEM((SEQS, TOK, CH), BF16),...  75 us
    unnamed x2, local copies, waits for them, and re-layouts  1.67 us

profile of v6, /device:TPU:1, one launch (start us, length us, event | category | flops | bytes accessed | tf_op | source)
XLA Modules:
  0.0 77.4 jit_solution(5584179021164804325)
XLA Ops:
  0.6 75.0 %shard_map.149 = (bf16[4,128,1024]{2,1,0:T(8,128)(2,1)S(1)}, f32[1,4,16,1024]{3,2,1,0:T(8,128)S(1)}) custom-call(bf16[3,4,1024]{2,1,0:T(4,128)(2,1)} %bitcast.6, f32[4,1024]{1,0:T(4,128)} %cw_hbm.1, f32[1,1024]{1,0:T(1,128)} %bitcast.7, bf16[32,1024]{1,0:T(8,128)(2,1)} %bitcast.5, f32[1,1024]{1,0:T(1,128)} %bitcast.8, f32[16,1024]{1,0:T(8,128)} %decay_hbm.1, ...), custom_call_target="tpu_custom_call" | custom-call | tf_op jit(solution)/shard_map/pallas_call | solution.py:665
  75.7 1.0 %copy.18 = bf16[4,128,1024]{2,1,0:T(8,128)(2,1)} copy(bf16[4,128,1024]{2,1,0:T(8,128)(2,1)S(1)} %get-tuple-element.2) | data formatting | bytes 2097152
  76.7 0.7 copy.19
